TPU v7x, 128 devices: a whole 4x4x4 slice. The times are simulated.
128 devices in a mesh: section: 4 (over x_hi, core), shard: 32 (over x_lo, z, y).
Axes of the slice: x: 4 (x_hi: 2, x_lo: 2; x = x_hi * 2 + x_lo), y: 4, z: 4, core: 2. Of those that a mesh axis runs over, the one named last changes fastest.
Arguments:
- hidden: bfloat16 [1024, 8192], P(('section', 'shard')), may hold values from -6 to 6
- norm_gain: float32 [4, 8192], P('section'), may hold values from 0.1 to 1.9
- gate_weight: bfloat16 [4, 8192, 16384], P('section', None, 'shard'), may hold values from -0.0625 to 0.0625
- up_weight: bfloat16 [4, 8192, 16384], P('section', None, 'shard'), may hold values from -0.0625 to 0.0625
- head_vector: bfloat16 [4, 16384], P('section', 'shard'), may hold values from -0.046875 to 0.046875
- pack_slot: int32 [4, 1024], replicated, may hold values from 0 to 1023, each once within a row
- owner_slot: int32 [1024], replicated, may hold values from 0 to 1023, each once
Outputs:
- section_scores: float32 [4, 1024], P('section', 'shard')
- joined: float32 [4, 1024], P(None, ('section', 'shard'))
All inputs are finite; a program needn't handle non-finite values.
Results may differ from a plain program's by a relative error of at most 0.0032.
Values may be sent and summed in bfloat16 or wider, within the bound.
No kernel may reach another device: no remote copies, remote signals or barrier semaphores. Data moves between devices by JAX's collectives and lax.ppermute only.
A program may use at most 128 MiB of HBM per device.

v0:
```python
import jax
import jax.numpy as jnp
from jax import lax
from jax.sharding import PartitionSpec as P

epsilon = 1e-06


def normalize(row_block, gain_row):
    widened = row_block.astype(jnp.float32)
    inv_rms = lax.rsqrt(jnp.mean(widened * widened, axis=1, keepdims=True) + epsilon)
    return (widened * inv_rms * gain_row).astype(jnp.bfloat16)


def score_block(normed, gate_cols, up_cols, head_cols):
    gate_out = jnp.dot(normed, gate_cols, preferred_element_type=jnp.float32)
    up_out = jnp.dot(normed, up_cols, preferred_element_type=jnp.float32)
    activated = jax.nn.silu(gate_out) * up_out
    return jnp.dot(activated, head_cols.astype(jnp.float32), precision=lax.Precision.HIGHEST)


def invert(ordering):
    total_rows = ordering.shape[0]
    return (
        jnp.zeros((total_rows,), jnp.int32)
        .at[ordering]
        .set(jnp.arange(total_rows, dtype=jnp.int32))
    )


def body(hidden, norm_gain, gate_weight, up_weight, head_vector, pack_slot, owner_slot):
    gain_row = norm_gain[0]
    gate_cols = gate_weight[0]
    up_cols = up_weight[0]
    head_cols = head_vector[0]
    partial_value = score_block(
        normalize(lax.all_gather(hidden, ("section", "shard"), axis=0, tiled=True), gain_row),
        gate_cols,
        up_cols,
        head_cols,
    )
    section = lax.axis_index("section")
    own_pack = lax.dynamic_index_in_dim(pack_slot, section, 0, keepdims=False)
    inverse = invert(own_pack)
    packed = partial_value[inverse]
    scores = lax.psum_scatter(packed, "shard", scatter_dimension=0, tiled=True)
    flipped = jnp.logical_or(section == 1, section == 3)
    values = jnp.where(flipped, jax.nn.log_sigmoid(scores), scores)
    shards = lax.axis_size("shard")
    sections = lax.axis_size("section")
    pack_rows = values.shape[0]
    total_rows = owner_slot.shape[0]
    own_count = total_rows // (shards * sections)
    first_row = lax.axis_index("shard") * pack_rows
    rows_here = lax.dynamic_slice_in_dim(inverse, first_row, pack_rows)
    targets = owner_slot[rows_here]
    spread = jnp.zeros((total_rows,), jnp.float32).at[targets].set(values)
    spread = spread.reshape(sections * shards, own_count)
    arrived = lax.all_to_all(spread, ("section", "shard"), split_axis=0, concat_axis=0, tiled=True)
    joined = arrived.reshape(sections, shards, own_count).sum(axis=1)
    return (values[None, :], joined)


def solution(mesh):
    in_specs = (
        P(("section", "shard"), None),
        P("section", None),
        P("section", None, "shard"),
        P("section", None, "shard"),
        P("section", "shard"),
        P(),
        P(),
    )
    out_specs = (P("section", "shard"), P(None, ("section", "shard")))
    return jax.shard_map(body, mesh=mesh, in_specs=in_specs, out_specs=out_specs, check_vma=False)
```

profile of v0, /device:TPU:1, one launch (start us, length us, event | category | flops | bytes accessed | tf_op | source)
XLA Modules:
  0.0 487.9 jit_solution(15857791865865555446)
XLA Ops:
  7.2 0.0 copy-start
  7.2 0.0 all-gather.2.cloned.1.call-start
  7.2 0.7 all-gather.2.cloned.1.call-update
  7.9 0.7 compare_select_fusion
  8.7 4.3 scatter_custom_fusion
  13.0 1.2 dynamic-slice
  14.9 0.1 compare_select_fusion.3
  15.0 0.0 copy-done
  15.0 0.0 copy-start.2
  15.0 0.7 gather_fusion.1
  15.7 324.4 %all-gather.2.cloned.1.call-done = bf16[1024,8192]{1,0:T(8,128)(2,1)} async-done(((bf16[8,8192]{1,0:T(8,128)(2,1)}), bf16[1024,8192]{1,0:T(8,128)(2,1)}) %all-gather.2.cloned.1.call-update) | async-done | bytes 16777232 | tf_op jit(solution)/shard_map/all_gather | solution.py:37
  340.1 0.0 copy-start.1
  340.1 7.5 %fusion = f32[1024]{0:T(1024)S(1)} fusion(bf16[1024,8192]{1,0:T(8,128)(2,1)} %all-gather.2.cloned.1.call-done), kind=kLoop, calls=%fused_computation.6 | loop fusion | flops 25164800 | bytes 16781312 | tf_op jit(solution)/shard_map/reduce_sum | solution.py:11
  347.7 0.0 copy-done.2
  347.7 3.1 copy-done.1
  350.8 12.7 %fusion.3 = f32[1024,512]{1,0:T(8,128)} fusion(bf16[1,8192,512]{2,1,0:T(8,128)(2,1)} %param.10, bf16[1024,8192]{1,0:T(8,128)(2,1)S(1)} %copy-done.1, f32[8192]{0:T(1024)S(1)} %bitcast.28, f32[1024]{0:T(1024)S(1)} %add_rsqrt_fusion), kind=kOutput, calls=%fused_computation.9 | convolution fusion | flops 8623489024 | bytes 27299840 | tf_op jit(solution)/shard_map/dot_general | solution.py:17
  363.5 0.0 copy-start.3
  363.5 12.7 %fusion.5 = f32[1024,512]{1,0:T(8,128)} fusion(bf16[1,8192,512]{2,1,0:T(8,128)(2,1)} %param.9, bf16[1024,8192]{1,0:T(8,128)(2,1)S(1)} %copy-done.1, f32[8192]{0:T(1024)S(1)} %bitcast.29, f32[1024]{0:T(1024)S(1)} %add_rsqrt_fusion), kind=kOutput, calls=%fused_computation.11 | convolution fusion | flops 8623489024 | bytes 27299840 | tf_op jit(solution)/shard_map/dot_general | solution.py:16
  376.2 0.0 copy-done.3
  376.2 3.7 fusion.9
  380.0 4.5 gather_fusion
  384.5 69.1 %all-reduce = f32[1024]{0:T(1024)S(1)} all-reduce(f32[1024]{0:T(1024)S(1)} %gather_fusion), channel_id=2, replica_groups=mesh['section'=4,'shard'=32] {'shard'}, use_global_device_ids=true, to_apply=%region_2.3.clone | all-reduce | flops 1024 | bytes 8192
  453.6 0.1 broadcast_select_fusion
  453.7 0.7 scatter_custom_fusion.1
  454.4 0.7 all_to_all.6
  455.1 15.7 %all-to-all-start = ((f32[128,1,8]{2,1,0:T(1,128)}), f32[128,1,8]{2,1,0:T(1,128)S(1)}, u32[]{:S(2)}, u32[]{:S(2)}) async-start(f32[128,1,8]{2,1,0:T(1,128)} %bitcast.9), calls=%async_computation | async-start | bytes 131072 | tf_op jit(solution)/shard_map/all_to_all | solution.py:59
  470.8 0.6 fusion.26
  471.4 9.0 %all-to-all-done = f32[128,1,8]{2,1,0:T(1,128)S(1)} async-done(((f32[128,1,8]{2,1,0:T(1,128)}), f32[128,1,8]{2,1,0:T(1,128)S(1)}, u32[]{:S(2)}, u32[]{:S(2)}) %all-to-all-start) | async-done | bytes 4128 | tf_op jit(solution)/shard_map/all_to_all | solution.py:59
  480.4 0.6 bitcast_reduce_fusion
  (5 shorter events, 0.0 us)
Async XLA Ops:
  7.2 7.8 %copy-start = (s32[1024]{0:T(1024)S(1)}, s32[1024]{0:T(1024)}, u32[]{:S(2)}) copy-start(s32[1024]{0:T(1024)} %param.13) | copy-start | bytes 12292
  7.2 333.0 %all-gather.2.cloned.1.call-start = ((), (), s32[]{:S(2)}) async-start(), calls=%async_computation.1 | async-start | bytes 16908288 | tf_op jit(solution)/shard_map/all_gather | solution.py:37
  15.0 332.7 %copy-start.2 = (f32[1,8192]{1,0:T(1,128)S(1)}, f32[1,8192]{1,0:T(1,128)}, u32[]{:S(2)}) copy-start(f32[1,8192]{1,0:T(1,128)} %param.8) | copy-start | bytes 98308
  340.1 10.7 %copy-start.1 = (bf16[1024,8192]{1,0:T(8,128)(2,1)S(1)}, bf16[1024,8192]{1,0:T(8,128)(2,1)}, u32[]{:S(2)}) copy-start(bf16[1024,8192]{1,0:T(8,128)(2,1)} %all-gather.2.cloned.1.call-done) | copy-start | bytes 50331652
  363.5 12.7 %copy-start.3 = (bf16[1,512]{1,0:T(2,128)(2,1)S(1)}, bf16[1,512]{1,0:T(2,128)(2,1)}, u32[]{:S(2)}) copy-start(bf16[1,512]{1,0:T(2,128)(2,1)} %param.11) | copy-start | bytes 3076
  455.1 25.3 %all-to-all-start = ((f32[128,1,8]{2,1,0:T(1,128)}), f32[128,1,8]{2,1,0:T(1,128)S(1)}, u32[]{:S(2)}, u32[]{:S(2)}) async-start(f32[128,1,8]{2,1,0:T(1,128)} %bitcast.9), calls=%async_computation | async-start | bytes 131072 | tf_op jit(solution)/shard_map/all_to_all | solution.py:59
Sparse Core Ops, SparseCore 0:
  9.7 330.3 all-gather.1
where the time goes:
time: 488 us
  waiting for transfers between devices  334 us (68%)
  blocking collectives  69.1 us (14%)
  matrix products  29.1 us (6%)
  starting transfers between devices  15.7 us (3%)
  local copies, waits for them, and re-layouts  15.3 us (3%)
  between operations  14.8 us (3%)
  other arithmetic  9.65 us (2%)
    all_gather x1, waiting for transfers between devices, body(): lax.all_gather(hidden, ('section', 'shard'), axis=0, tiled=True)  324 us
    unnamed x1, blocking collectives  69.1 us
    all_to_all x1, starting transfers between devices, body(): lax.all_to_all(spread, ('section', 'shard'), split_axis=0, concat_axis=0,...  15.7 us
    dot_general x1, matrix products, score_block(): up_out = jnp.dot(normed, up_cols, preferred_element_type=jnp.float32)  12.7 us
    dot_general x1, matrix products, score_block(): gate_out = jnp.dot(normed, gate_cols, preferred_element_type=jnp.float32)  12.7 us
  transfers between devices with their start and end apart: 2, of which 2 were waited for; matrix products, arithmetic and copies ran while one was open for 2% of the time, Pallas kernels for 0%

commit v1 on v0

v1 whole, which is shorter than its diff:
```python
import functools

import jax
import jax.numpy as jnp
from jax import lax
from jax.experimental import pallas as pl
from jax.experimental.pallas import tpu as pltpu
from jax.sharding import Mesh, PartitionSpec as P

epsilon = 1e-06
ALL = ("xh", "core", "xl", "z", "y")
ORDER = (("y", "x", "z"), ("x", "z", "y"))
ROWS = 256
STEP = 1024


def flat_index(x, y, z, core):
    return (x // 2) * 64 + core * 32 + (x % 2) * 16 + z * 4 + y


def shift_pairs(phase, step):
    pairs = []
    for core in range(2):
        at = "xyz".index(ORDER[core][phase])
        for x in range(4):
            for y in range(4):
                for z in range(4):
                    to = [x, y, z]
                    to[at] = (to[at] + step) % 4
                    pairs.append((flat_index(x, y, z, core), flat_index(*to, core)))
    return pairs


def shift(block, phase, step):
    return lax.ppermute(block, ALL, shift_pairs(phase, step))


def sibling(block):
    return lax.ppermute(block, "core", [(0, 1), (1, 0)])


def stage_kernel(pieces, features, *refs):
    rows = refs[:pieces]
    gate_ref, up_ref, head_ref, column_ref, row_ref, before_ref, out_ref, gate_sum, up_sum, square_sum = refs[pieces:]
    step = pl.program_id(0)

    @pl.when(step == 0)
    def _():
        gate_sum[...] = jnp.zeros_like(gate_sum)
        up_sum[...] = jnp.zeros_like(up_sum)
        square_sum[...] = jnp.zeros_like(square_sum)

    block = jnp.concatenate([ref[...] for ref in rows], axis=0)
    gate_sum[...] += jnp.dot(block, gate_ref[...], preferred_element_type=jnp.float32)
    up_sum[...] += jnp.dot(block, up_ref[...], preferred_element_type=jnp.float32)
    total = square_sum[...]
    for at in range(0, STEP, 128):
        part = block[:, at : at + 128].astype(jnp.float32)
        total = total + part * part
    square_sum[...] = total

    @pl.when(step == pl.num_programs(0) - 1)
    def _():
        mean = jnp.sum(square_sum[...], axis=1, keepdims=True) / features
        inv_rms = lax.rsqrt(mean + epsilon)
        gate = gate_sum[...] * inv_rms
        up = up_sum[...] * inv_rms
        activated = gate / (1.0 + jnp.exp(-gate)) * up
        score = jnp.sum(activated * head_ref[...], axis=1, keepdims=True)
        lane = lax.broadcasted_iota(jnp.int32, (ROWS, 128), 1)
        line = lax.broadcasted_iota(jnp.int32, (128, ROWS), 0)
        owner_part = jnp.where(column_ref[:, 0:1] == lane, score, 0.0)
        pack_part = jnp.where(column_ref[:, 1:2] == lane, score, 0.0)
        owner_line = jnp.where(row_ref[0:1, :] == line, 1.0, 0.0)
        pack_line = jnp.where(row_ref[1:2, :] == line, 1.0, 0.0)
        out_ref[...] = (
            before_ref[...]
            + jnp.dot(owner_line, owner_part, precision=lax.Precision.HIGHEST, preferred_element_type=jnp.float32)
            + jnp.dot(pack_line, pack_part, precision=lax.Precision.HIGHEST, preferred_element_type=jnp.float32)
        )


def stage(rows, gate, up, head, column, row, before):
    features, width = gate.shape
    return pl.pallas_call(
        functools.partial(stage_kernel, len(rows), features),
        grid=(features // STEP,),
        out_shape=jax.ShapeDtypeStruct((128, 128), jnp.float32),
        in_specs=[pl.BlockSpec((piece.shape[0], STEP), lambda k: (0, k)) for piece in rows]
        + [pl.BlockSpec((STEP, width), lambda k: (k, 0))] * 2
        + [
            pl.BlockSpec((1, width), lambda k: (0, 0)),
            pl.BlockSpec(column.shape, lambda k: (0, 0)),
            pl.BlockSpec(row.shape, lambda k: (0, 0)),
            pl.BlockSpec((128, 128), lambda k: (0, 0)),
        ],
        out_specs=pl.BlockSpec((128, 128), lambda k: (0, 0)),
        scratch_shapes=[
            pltpu.VMEM((ROWS, width), jnp.float32),
            pltpu.VMEM((ROWS, width), jnp.float32),
            pltpu.VMEM((ROWS, 128), jnp.float32),
        ],
        compiler_params=pltpu.CompilerParams(vmem_limit_bytes=32 * 1024 * 1024),
        cost_estimate=pl.CostEstimate(flops=4 * ROWS * features * width, bytes_accessed=4 * features * width, transcendentals=ROWS * width),
    )(*rows, gate, up, head, column, row, before)


def tokens_of(core, third):
    place = {"x": lax.axis_index("xh") * 2 + lax.axis_index("xl"), "y": lax.axis_index("y"), "z": lax.axis_index("z")}
    at = jnp.arange(128, dtype=jnp.int32)
    back = (at // 8 % 4, at // 32, third)
    token = []
    for half in range(2):
        source = {axis: (place[axis] - back[phase]) % 4 for phase, axis in enumerate(ORDER[half])}
        token.append(flat_index(source["x"], source["y"], source["z"], half) * 8 + at % 8)
    return jnp.where(core == 0, token[0], token[1])


def body(hidden, norm_gain, gate_weight, up_weight, head_vector, pack_slot, owner_slot):
    core = lax.axis_index("core")
    section = lax.axis_index("xh") * 2 + core
    gain = norm_gain[0][:, None]
    gate = (gate_weight[0].astype(jnp.float32) * gain).astype(jnp.bfloat16)
    up = (up_weight[0].astype(jnp.float32) * gain).astype(jnp.bfloat16)
    head = head_vector.astype(jnp.float32)
    own_pack = lax.dynamic_index_in_dim(pack_slot, section, 0, keepdims=False)

    line = jnp.concatenate([hidden] + [shift(hidden, 0, step) for step in (1, 2, 3)], axis=0)
    plane = jnp.concatenate([line] + [shift(line, 1, step) for step in (1, 2, 3)], axis=0)
    behind = shift(plane, 2, 1)
    ahead = shift(plane, 2, 3)
    far_low = shift(behind[:64], 2, 1)
    far_high = shift(ahead[64:], 2, 3)
    groups = ((0, (plane,)), (1, (behind,)), (3, (ahead,)), (2, (far_low, far_high)))

    sent = jnp.zeros((128, 128), jnp.float32)
    for third, pieces in groups:
        rows = list(pieces) + [sibling(piece) for piece in pieces]
        token = jnp.concatenate([tokens_of(core, third), tokens_of(1 - core, third)])
        owner, pack = owner_slot[token], own_pack[token]
        column = jnp.stack([owner % 8, pack % 32 + 8], axis=1)
        row = jnp.stack([owner // 8, pack // 32 + 32 * section], axis=0)
        sent = stage(rows, gate, up, head, column, row, sent)

    arrived = lax.all_to_all(sent[:, None, :], ALL, split_axis=0, concat_axis=0, tiled=True)
    sums = arrived.reshape(4, 32, 128).sum(axis=1)
    flipped = lax.broadcasted_iota(jnp.int32, (4, 8), 0) % 2 == 1
    joined = sums[:, :8]
    joined = jnp.where(flipped, jax.nn.log_sigmoid(joined), joined)
    scores = sums[:, 8:40].sum(axis=0, keepdims=True)
    scores = jnp.where(section % 2 == 1, jax.nn.log_sigmoid(scores), scores)
    return scores, joined


def solution(mesh):
    parts = Mesh(mesh.devices.reshape(2, 2, 2, 4, 4), ALL)
    section, shard = ("xh", "core"), ("xl", "z", "y")
    in_specs = (
        P(section + shard, None),
        P(section, None),
        P(section, None, shard),
        P(section, None, shard),
        P(section, shard),
        P(),
        P(),
    )
    out_specs = (P(section, shard), P(None, section + shard))
    return jax.shard_map(body, mesh=parts, in_specs=in_specs, out_specs=out_specs, check_vma=False)
```

time: 488 us -> 173 us (0.35)
  waiting for transfers between devices: 334 us -> 42.8 us
  blocking collectives: 69.1 us -> 0 us
  Pallas kernels: 0 us -> 34.8 us
  matrix products: 29.1 us -> 0 us
  local copies, waits for them, and re-layouts: 15.3 us -> 38 us
  starting transfers between devices: 15.7 us -> 34.5 us
  between operations: 14.8 us -> 1.11 us
  other arithmetic: 9.65 us -> 21.3 us
    all_gather x1 -> x0, waiting for transfers between devices: 324 us -> none  [body(): lax.all_gather(hidden, ('section', 'shard'), axis=0, tiled=True)]
    unnamed x1 -> x0, blocking collectives: 69.1 us -> none
    pallas_call x0 -> x4, Pallas kernels: none -> 34.8 us  [stage(): pl.pallas_call(functools.partial(stage_kernel, len(rows), features), grid...]
    ppermute x0 -> x15, waiting for transfers between devices: none -> 33.3 us  [the longest x10 33.3 us: shift(): return lax.ppermute(block, ALL, shift_pairs(phase, step))]
    dot_general x3 -> x0, matrix products: 29.1 us -> none  [the longest x1 12.7 us: score_block(): up_out = jnp.dot(normed, up_cols, preferred_element_type=jnp.float32)]
    ppermute x0 -> x15, starting transfers between devices: none -> 26.5 us  [the longest x10 16.8 us: shift(): return lax.ppermute(block, ALL, shift_pairs(phase, step))]
    unnamed x9 -> x37, local copies, waits for them, and re-layouts: 4.38 us -> 20.4 us
    convert_element_type x0 -> x2, other arithmetic: none -> 12.8 us  [the longest x1 12.3 us: body(): up = (up_weight[0].astype(jnp.float32) * gain).astype(jnp.bfloat16)]
  transfers between devices with their start and end apart: 2 -> 16, of which waited for: 2 -> 7; matrix products, arithmetic and copies ran while one was open for 2% -> 24% of each run, Pallas kernels for 0% -> 15%
where the time goes in v1:
time: 173 us; the launch traced here: 172 us
  waiting for transfers between devices  42.8 us (25%)
  local copies, waits for them, and re-layouts  38 us (22%)
  Pallas kernels  34.8 us (20%)
  starting transfers between devices  34.5 us (20%)
  other arithmetic  21.3 us (12%)
    pallas_call x4, Pallas kernels, stage(): pl.pallas_call(functools.partial(stage_kernel, len(rows), features), grid...  34.8 us
    ppermute x10, waiting for transfers between devices, shift(): return lax.ppermute(block, ALL, shift_pairs(phase, step))  33.3 us
    unnamed x37, local copies, waits for them, and re-layouts  20.4 us
    ppermute x10, starting transfers between devices, shift(): return lax.ppermute(block, ALL, shift_pairs(phase, step))  16.8 us
    convert_element_type x1, other arithmetic, body(): up = (up_weight[0].astype(jnp.float32) * gain).astype(jnp.bfloat16)  12.3 us
    gather x8, local copies, waits for them, and re-layouts, body(): owner, pack = (owner_slot[token], own_pack[token])  10.9 us
    ppermute x5, starting transfers between devices, sibling(): return lax.ppermute(block, 'core', [(0, 1), (1, 0)])  9.71 us
    all_to_all x1, waiting for transfers between devices, body(): lax.all_to_all(sent[:, None, :], ALL, split_axis=0, concat_axis=0, tiled=...  9.49 us
  transfers between devices with their start and end apart: 16, of which 7 were waited for; matrix products, arithmetic and copies ran while one was open for 24% of the time, Pallas kernels for 15%

profile of v1, /device:TPU:1, one launch (start us, length us, event | category | flops | bytes accessed | tf_op | source)
XLA Modules:
  0.0 172.5 jit_solution(5783492290840774023)
XLA Ops:
  0.6 2.1 %collective-permute-start = (bf16[8,8192]{1,0:T(8,128)(2,1)}, bf16[8,8192]{1,0:T(8,128)(2,1)S(1)}, u32[]{:S(2)}, u32[]{:S(2)}) collective-permute-start(bf16[8,8192]{1,0:T(8,128)(2,1)} %param.7), channel_id=1, source_target_pairs={{0,1},{4,5},{8,9},{12,13},{1,2},{5,6},{9,10},{13,14},{2,3},{6,7},{... | collective-permute-start | bytes 393224 | tf_op jit(solution)/shard_map/ppermute | solution.py:35
  2.8 2.5 %collective-permute-start.1 = (bf16[8,8192]{1,0:T(8,128)(2,1)}, bf16[8,8192]{1,0:T(8,128)(2,1)S(1)}, u32[]{:S(2)}, u32[]{:S(2)}) collective-permute-start(bf16[8,8192]{1,0:T(8,128)(2,1)} %param.7), channel_id=1, source_target_pairs={{0,2},{4,6},{8,10},{12,14},{1,3},{5,7},{9,11},{13,15},{2,0},{6,4},... | collective-permute-start | bytes 393224 | tf_op jit(solution)/shard_map/ppermute | solution.py:35
  5.2 1.2 collective-permute-start.2
  6.4 1.6 constant_dynamic-update-slice_fusion.3
  8.2 1.4 gather_fusion.7
  9.6 12.3 %fusion = (bf16[8192,512]{1,0:T(8,128)(2,1)}, bf16[8192,512]{1,0:T(8,128)(2,1)}) fusion(bf16[1,8192,512]{2,1,0:T(8,128)(2,1)} %param.10, f32[8192]{0:T(1024)} %bitcast.60, bf16[1,8192,512]{2,1,0:T(8,128)(2,1)} %param.9), kind=kLoop, calls=%fused_computation.9 | loop fusion | flops 25165824 | bytes 33587200 | tf_op jit(solution)/shard_map/convert_element_type | solution.py:124
  21.9 1.4 gather_fusion.6
  23.3 1.4 gather_fusion.5
  24.7 1.4 gather_fusion.4
  26.0 1.4 gather_fusion.3
  27.4 1.4 gather_fusion.2
  30.8 1.6 collective-permute-start.3
  32.5 1.4 gather_fusion.1
  33.9 1.4 gather_fusion
  35.3 3.4 %collective-permute-start.4 = (bf16[32,8192]{1,0:T(8,128)(2,1)S(1)}, bf16[32,8192]{1,0:T(8,128)(2,1)S(1)}, u32[]{:S(2)}, u32[]{:S(2)}) collective-permute-start(bf16[32,8192]{1,0:T(8,128)(2,1)S(1)} %get-tuple-element.2), channel_id=1, source_target_pairs={{0,64},{4,68},{8,72},{12,76},{1,65},{5,69},{9,73},{13,77},{2,66},{... | collective-permute-start | bytes 1572872 | tf_op jit(solution)/shard_map/ppermute | solution.py:35
  38.7 0.7 collective-permute-start.5
  39.4 2.1 %collective-permute-done.3 = bf16[32,8192]{1,0:T(8,128)(2,1)S(1)} collective-permute-done((bf16[32,8192]{1,0:T(8,128)(2,1)S(1)}, bf16[32,8192]{1,0:T(8,128)(2,1)S(1)}, u32[]{:S(2)}, u32[]{:S(2)}) %collective-permute-start.3) | collective-permute-done | bytes 524320 | tf_op jit(solution)/shard_map/ppermute | solution.py:35
  41.5 0.8 constant_dynamic-update-slice_fusion.6
  42.3 6.0 %collective-permute-done.4 = bf16[32,8192]{1,0:T(8,128)(2,1)S(1)} collective-permute-done((bf16[32,8192]{1,0:T(8,128)(2,1)S(1)}, bf16[32,8192]{1,0:T(8,128)(2,1)S(1)}, u32[]{:S(2)}, u32[]{:S(2)}) %collective-permute-start.4) | collective-permute-done | bytes 524320 | tf_op jit(solution)/shard_map/ppermute | solution.py:35
  48.3 0.8 constant_dynamic-update-slice_fusion.5
  49.1 1.5 collective-permute-done.5
  50.6 0.9 constant_dynamic-update-slice_fusion.4.refs_0_
  51.4 1.3 collective-permute-start.6
  53.3 1.4 collective-permute-start.8
  55.4 3.2 %collective-permute-start.14 = (bf16[128,8192]{1,0:T(8,128)(2,1)}, bf16[128,8192]{1,0:T(8,128)(2,1)}, u32[]{:S(2)}, u32[]{:S(2)}) collective-permute-start(bf16[128,8192]{1,0:T(8,128)(2,1)} %constant_dynamic-update-slice_fusion.4.refs_0_), channel_id=1, source_target_pairs={{0,32},{32,0},{1,33},{33,1},{2,34},{34,2},{3,35},{35,3},{4,36},{36... | collective-permute-start | bytes 6291464 | tf_op jit(solution)/shard_map/ppermute | solution.py:39
  58.6 19.5 %collective-permute-done.6.refs_0_ = bf16[128,8192]{1,0:T(8,128)(2,1)S(1)} collective-permute-done((bf16[128,8192]{1,0:T(8,128)(2,1)}, bf16[128,8192]{1,0:T(8,128)(2,1)S(1)}, u32[]{:S(2)}, u32[]{:S(2)}) %collective-permute-start.6) | collective-permute-done | bytes 2097184 | tf_op jit(solution)/shard_map/ppermute | solution.py:35
  78.0 3.4 %collective-permute-start.13 = (bf16[128,8192]{1,0:T(8,128)(2,1)S(1)}, bf16[128,8192]{1,0:T(8,128)(2,1)}, u32[]{:S(2)}, u32[]{:S(2)}) collective-permute-start(bf16[128,8192]{1,0:T(8,128)(2,1)S(1)} %collective-permute-done.6.refs_0_), channel_id=1, source_target_pairs={{0,32},{32,0},{1,33},{33,1},{2,34},{34,2},{3,35},{35,3},{4,36},{36... | collective-permute-start | bytes 6291464 | tf_op jit(solution)/shard_map/ppermute | solution.py:39
  83.2 1.1 slice.32
  84.7 2.3 %slice.33 = bf16[64,8192]{1,0:T(8,128)(2,1)} slice(bf16[128,8192]{1,0:T(8,128)(2,1)} %collective-permute-done.8.refs_0_), slice={[64:128], [0:8192]} | slice | bytes 2097152 | tf_op jit(solution)/shard_map/slice | solution.py:133
  86.9 2.3 %collective-permute-start.9 = (bf16[64,8192]{1,0:T(8,128)(2,1)}, bf16[64,8192]{1,0:T(8,128)(2,1)}, u32[]{:S(2)}, u32[]{:S(2)}) collective-permute-start(bf16[64,8192]{1,0:T(8,128)(2,1)} %slice.33), channel_id=1, source_target_pairs={{0,12},{4,0},{8,4},{12,8},{1,13},{5,1},{9,5},{13,9},{2,14},{6,2},{... | collective-permute-start | bytes 3145736 | tf_op jit(solution)/shard_map/ppermute | solution.py:35
  89.8 0.8 copy.49.refs_5_
  91.5 0.8 copy.52.refs_7_
  92.9 0.7 and_select_fusion.9
  93.6 0.7 pad_add_fusion.3.refs_6_
  95.7 4.0 %collective-permute-done.7.refs_0_ = bf16[64,8192]{1,0:T(8,128)(2,1)S(1)} collective-permute-done((bf16[64,8192]{1,0:T(8,128)(2,1)}, bf16[64,8192]{1,0:T(8,128)(2,1)S(1)}, u32[]{:S(2)}, u32[]{:S(2)}) %collective-permute-start.7) | collective-permute-done | bytes 1048608 | tf_op jit(solution)/shard_map/ppermute | solution.py:35
  99.6 1.4 collective-permute-start.10
  101.3 1.8 %collective-permute-start.11 = (bf16[64,8192]{1,0:T(8,128)(2,1)}, bf16[64,8192]{1,0:T(8,128)(2,1)S(1)}, u32[]{:S(2)}, u32[]{:S(2)}) collective-permute-start(bf16[64,8192]{1,0:T(8,128)(2,1)} %collective-permute-done.9.refs_1_), channel_id=1, source_target_pairs={{0,32},{32,0},{1,33},{33,1},{2,34},{34,2},{3,35},{35,3},{4,36},{36... | collective-permute-start | bytes 3145736 | tf_op jit(solution)/shard_map/ppermute | solution.py:39
  103.1 3.4 %copy-done.1 = bf16[8192,512]{1,0:T(8,128)(2,1)S(1)} copy-done((bf16[8192,512]{1,0:T(8,128)(2,1)S(1)}, bf16[8192,512]{1,0:T(8,128)(2,1)}, u32[]{:S(2)}) %copy-start.1) | copy-done | bytes 8388632
  106.4 3.4 %copy-done.3 = bf16[8192,512]{1,0:T(8,128)(2,1)S(1)} copy-done((bf16[8192,512]{1,0:T(8,128)(2,1)S(1)}, bf16[8192,512]{1,0:T(8,128)(2,1)}, u32[]{:S(2)}) %copy-start.3) | copy-done | bytes 8388632
  109.8 0.9 copy-done.5
  112.1 8.7 %shard_map.86.refs_7_ = f32[128,128]{1,0:T(8,128)S(1)} custom-call(bf16[128,8192]{1,0:T(8,128)(2,1)} %constant_dynamic-update-slice_fusion.4.refs_0_, bf16[128,8192]{1,0:T(8,128)(2,1)} %collective-permute-done.14.refs_1_, bf16[8192,512]{1,0:T(8,128)(2,1)S(1)} %copy-done.3, bf16[8192,512]{1,0:T(8,128)(2,1)S(1)} %copy-done.1, f32[1,512]{1,0:T(1,128)S(1)} %copy-done.6, ...), custom_call_target="tpu_custom_call" | custom-call | flops 4294967296 | bytes 16777216 | tf_op jit(solution)/shard_map/pallas_call | solution.py:85
  120.9 3.4 %copy-done.2 = bf16[8192,512]{1,0:T(8,128)(2,1)S(1)} copy-done((bf16[8192,512]{1,0:T(8,128)(2,1)S(1)}, bf16[8192,512]{1,0:T(8,128)(2,1)}, u32[]{:S(2)}) %copy-start.2) | copy-done | bytes 8388632
  124.2 3.4 %copy-done.4 = bf16[8192,512]{1,0:T(8,128)(2,1)S(1)} copy-done((bf16[8192,512]{1,0:T(8,128)(2,1)S(1)}, bf16[8192,512]{1,0:T(8,128)(2,1)}, u32[]{:S(2)}) %copy-start.4) | copy-done | bytes 8388632
  127.6 8.4 %shard_map.87.refs_7_ = f32[128,128]{1,0:T(8,128)S(1)} custom-call(bf16[128,8192]{1,0:T(8,128)(2,1)S(1)} %collective-permute-done.6.refs_0_, bf16[128,8192]{1,0:T(8,128)(2,1)} %collective-permute-done.13.refs_1_, bf16[8192,512]{1,0:T(8,128)(2,1)S(1)} %copy-done.4, bf16[8192,512]{1,0:T(8,128)(2,1)S(1)} %copy-done.2, f32[1,512]{1,0:T(1,128)S(1)} %copy-done.7, ...), custom_call_target="tpu_custom_call" | custom-call | flops 4294967296 | bytes 16777216 | tf_op jit(solution)/shard_map/pallas_call | solution.py:85
  136.0 8.7 %shard_map.88.refs_9_ = f32[128,128]{1,0:T(8,128)S(1)} custom-call(bf16[128,8192]{1,0:T(8,128)(2,1)} %collective-permute-done.8.refs_0_, bf16[128,8192]{1,0:T(8,128)(2,1)} %collective-permute-done.12.refs_1_, bf16[8192,512]{1,0:T(8,128)(2,1)S(1)} %copy-done.4, bf16[8192,512]{1,0:T(8,128)(2,1)S(1)} %copy-done.2, f32[1,512]{1,0:T(1,128)S(1)} %copy-done.7, ...), custom_call_target="tpu_custom_call" | custom-call | flops 4294967296 | bytes 16777216 | tf_op jit(solution)/shard_map/pallas_call | solution.py:85
  144.8 8.9 %shard_map.89 = f32[128,128]{1,0:T(8,128)} custom-call(bf16[64,8192]{1,0:T(8,128)(2,1)S(1)} %collective-permute-done.7.refs_0_, bf16[64,8192]{1,0:T(8,128)(2,1)} %collective-permute-done.9.refs_1_, bf16[64,8192]{1,0:T(8,128)(2,1)S(1)} %collective-permute-done.10.refs_2_, bf16[64,8192]{1,0:T(8,128)(2,1)S(1)} %collective-permute-done.11.refs_3_, ...), custom_call_target="tpu_custom_call" | custom-call | flops 4294967296 | bytes 16777216 | tf_op jit(solution)/shard_map/pallas_call | solution.py:85
  153.7 8.0 %all-to-all-start = ((f32[128,1,128]{2,1,0:T(1,128)}), f32[128,1,128]{2,1,0:T(1,128)S(1)}, u32[]{:S(2)}, u32[]{:S(2)}) async-start(f32[128,1,128]{2,1,0:T(1,128)} %bitcast.33), calls=%async_computation | async-start | bytes 131072 | tf_op jit(solution)/shard_map/all_to_all | solution.py:145
  161.7 9.5 %all-to-all-done = f32[128,1,128]{2,1,0:T(1,128)S(1)} async-done(((f32[128,1,128]{2,1,0:T(1,128)}), f32[128,1,128]{2,1,0:T(1,128)S(1)}, u32[]{:S(2)}, u32[]{:S(2)}) %all-to-all-start) | async-done | bytes 65568 | tf_op jit(solution)/shard_map/all_to_all | solution.py:145
  (87 shorter events, 12.1 us)
Async XLA Ops:
  0.6 7.5 %copy-start = (s32[4,1024]{1,0:T(4,128)S(1)}, s32[4,1024]{1,0:T(4,128)}, u32[]{:S(2)}) copy-start(s32[4,1024]{1,0:T(4,128)} %param.12) | copy-start | bytes 49156
  0.6 28.2 %collective-permute-start = (bf16[8,8192]{1,0:T(8,128)(2,1)}, bf16[8,8192]{1,0:T(8,128)(2,1)S(1)}, u32[]{:S(2)}, u32[]{:S(2)}) collective-permute-start(bf16[8,8192]{1,0:T(8,128)(2,1)} %param.7), channel_id=1, source_target_pairs={{0,1},{4,5},{8,9},{12,13},{1,2},{5,6},{9,10},{13,14},{2,3},{6,7},{... | collective-permute-start | bytes 393224 | tf_op jit(solution)/shard_map/ppermute | solution.py:35
  2.8 26.7 %collective-permute-start.1 = (bf16[8,8192]{1,0:T(8,128)(2,1)}, bf16[8,8192]{1,0:T(8,128)(2,1)S(1)}, u32[]{:S(2)}, u32[]{:S(2)}) collective-permute-start(bf16[8,8192]{1,0:T(8,128)(2,1)} %param.7), channel_id=1, source_target_pairs={{0,2},{4,6},{8,10},{12,14},{1,3},{5,7},{9,11},{13,15},{2,0},{6,4},... | collective-permute-start | bytes 393224 | tf_op jit(solution)/shard_map/ppermute | solution.py:35
  5.2 25.0 %collective-permute-start.2 = (bf16[8,8192]{1,0:T(8,128)(2,1)}, bf16[8,8192]{1,0:T(8,128)(2,1)S(1)}, u32[]{:S(2)}, u32[]{:S(2)}) collective-permute-start(bf16[8,8192]{1,0:T(8,128)(2,1)} %param.7), channel_id=1, source_target_pairs={{0,3},{4,7},{8,11},{12,15},{1,0},{5,4},{9,8},{13,12},{2,1},{6,5},{... | collective-permute-start | bytes 393224 | tf_op jit(solution)/shard_map/ppermute | solution.py:35
  9.6 12.3 %copy-start.9 = (s32[1024]{0:T(1024)S(1)}, s32[1024]{0:T(1024)}, u32[]{:S(2)}) copy-start(s32[1024]{0:T(1024)} %param.13) | copy-start | bytes 12292
  28.8 26.5 %copy-start.10 = (s32[256]{0:T(256)}, s32[256]{0:T(256)S(1)}, u32[]{:S(2)}) copy-start(s32[256]{0:T(256)S(1)} %gather_fusion.2) | copy-start | bytes 3076
  30.8 10.6 %collective-permute-start.3 = (bf16[32,8192]{1,0:T(8,128)(2,1)S(1)}, bf16[32,8192]{1,0:T(8,128)(2,1)S(1)}, u32[]{:S(2)}, u32[]{:S(2)}) collective-permute-start(bf16[32,8192]{1,0:T(8,128)(2,1)S(1)} %get-tuple-element.2), channel_id=1, source_target_pairs={{0,16},{4,20},{8,24},{12,28},{1,17},{5,21},{9,25},{13,29},{2,18},{... | collective-permute-start | bytes 1572872 | tf_op jit(solution)/shard_map/ppermute | solution.py:35
  33.9 21.5 %copy-start.12 = (s32[256]{0:T(256)}, s32[256]{0:T(256)S(1)}, u32[]{:S(2)}) copy-start(s32[256]{0:T(256)S(1)} %gather_fusion.1) | copy-start | bytes 3076
  35.2 47.9 %copy-start.11 = (s32[256]{0:T(256)}, s32[256]{0:T(256)S(1)}, u32[]{:S(2)}) copy-start(s32[256]{0:T(256)S(1)} %gather_fusion) | copy-start | bytes 3076
  35.3 13.0 %collective-permute-start.4 = (bf16[32,8192]{1,0:T(8,128)(2,1)S(1)}, bf16[32,8192]{1,0:T(8,128)(2,1)S(1)}, u32[]{:S(2)}, u32[]{:S(2)}) collective-permute-start(bf16[32,8192]{1,0:T(8,128)(2,1)S(1)} %get-tuple-element.2), channel_id=1, source_target_pairs={{0,64},{4,68},{8,72},{12,76},{1,65},{5,69},{9,73},{13,77},{2,66},{... | collective-permute-start | bytes 1572872 | tf_op jit(solution)/shard_map/ppermute | solution.py:35
  38.7 11.9 %collective-permute-start.5 = (bf16[32,8192]{1,0:T(8,128)(2,1)S(1)}, bf16[32,8192]{1,0:T(8,128)(2,1)S(1)}, u32[]{:S(2)}, u32[]{:S(2)}) collective-permute-start(bf16[32,8192]{1,0:T(8,128)(2,1)S(1)} %get-tuple-element.2), channel_id=1, source_target_pairs={{0,80},{4,84},{8,88},{12,92},{1,81},{5,85},{9,89},{13,93},{2,82},{... | collective-permute-start | bytes 1572872 | tf_op jit(solution)/shard_map/ppermute | solution.py:35
  51.4 26.6 %collective-permute-start.6 = (bf16[128,8192]{1,0:T(8,128)(2,1)}, bf16[128,8192]{1,0:T(8,128)(2,1)S(1)}, u32[]{:S(2)}, u32[]{:S(2)}) collective-permute-start(bf16[128,8192]{1,0:T(8,128)(2,1)} %constant_dynamic-update-slice_fusion.4.refs_0_), channel_id=1, source_target_pairs={{0,4},{4,8},{8,12},{12,0},{1,5},{5,9},{9,13},{13,1},{2,6},{6,10},{... | collective-permute-start | bytes 6291464 | tf_op jit(solution)/shard_map/ppermute | solution.py:35
  53.3 29.2 %collective-permute-start.8 = (bf16[128,8192]{1,0:T(8,128)(2,1)}, bf16[128,8192]{1,0:T(8,128)(2,1)}, u32[]{:S(2)}, u32[]{:S(2)}) collective-permute-start(bf16[128,8192]{1,0:T(8,128)(2,1)} %constant_dynamic-update-slice_fusion.4.refs_0_), channel_id=1, source_target_pairs={{0,12},{4,0},{8,4},{12,8},{1,13},{5,1},{9,5},{13,9},{2,14},{6,2},{... | collective-permute-start | bytes 6291464 | tf_op jit(solution)/shard_map/ppermute | solution.py:35
  55.4 47.7 %collective-permute-start.14 = (bf16[128,8192]{1,0:T(8,128)(2,1)}, bf16[128,8192]{1,0:T(8,128)(2,1)}, u32[]{:S(2)}, u32[]{:S(2)}) collective-permute-start(bf16[128,8192]{1,0:T(8,128)(2,1)} %constant_dynamic-update-slice_fusion.4.refs_0_), channel_id=1, source_target_pairs={{0,32},{32,0},{1,33},{33,1},{2,34},{34,2},{3,35},{35,3},{4,36},{36... | collective-permute-start | bytes 6291464 | tf_op jit(solution)/shard_map/ppermute | solution.py:39
  78.0 42.8 %collective-permute-start.13 = (bf16[128,8192]{1,0:T(8,128)(2,1)S(1)}, bf16[128,8192]{1,0:T(8,128)(2,1)}, u32[]{:S(2)}, u32[]{:S(2)}) collective-permute-start(bf16[128,8192]{1,0:T(8,128)(2,1)S(1)} %collective-permute-done.6.refs_0_), channel_id=1, source_target_pairs={{0,32},{32,0},{1,33},{33,1},{2,34},{34,2},{3,35},{35,3},{4,36},{36... | collective-permute-start | bytes 6291464 | tf_op jit(solution)/shard_map/ppermute | solution.py:39
  82.6 53.5 %collective-permute-start.12 = (bf16[128,8192]{1,0:T(8,128)(2,1)}, bf16[128,8192]{1,0:T(8,128)(2,1)}, u32[]{:S(2)}, u32[]{:S(2)}) collective-permute-start(bf16[128,8192]{1,0:T(8,128)(2,1)} %collective-permute-done.8.refs_0_), channel_id=1, source_target_pairs={{0,32},{32,0},{1,33},{33,1},{2,34},{34,2},{3,35},{35,3},{4,36},{36... | collective-permute-start | bytes 6291464 | tf_op jit(solution)/shard_map/ppermute | solution.py:39
  83.2 7.4 %copy-start.13 = (bf16[1,512]{1,0:T(2,128)(2,1)S(1)}, bf16[1,512]{1,0:T(2,128)(2,1)}, u32[]{:S(2)}) copy-start(bf16[1,512]{1,0:T(2,128)(2,1)} %param.11) | copy-start | bytes 3076
  84.3 15.4 %collective-permute-start.7 = (bf16[64,8192]{1,0:T(8,128)(2,1)}, bf16[64,8192]{1,0:T(8,128)(2,1)S(1)}, u32[]{:S(2)}, u32[]{:S(2)}) collective-permute-start(bf16[64,8192]{1,0:T(8,128)(2,1)} %slice.32), channel_id=1, source_target_pairs={{0,4},{4,8},{8,12},{12,0},{1,5},{5,9},{9,13},{13,1},{2,6},{6,10},{... | collective-permute-start | bytes 3145736 | tf_op jit(solution)/shard_map/ppermute | solution.py:35
  86.9 14.3 %collective-permute-start.9 = (bf16[64,8192]{1,0:T(8,128)(2,1)}, bf16[64,8192]{1,0:T(8,128)(2,1)}, u32[]{:S(2)}, u32[]{:S(2)}) collective-permute-start(bf16[64,8192]{1,0:T(8,128)(2,1)} %slice.33), channel_id=1, source_target_pairs={{0,12},{4,0},{8,4},{12,8},{1,13},{5,1},{9,5},{13,9},{2,14},{6,2},{... | collective-permute-start | bytes 3145736 | tf_op jit(solution)/shard_map/ppermute | solution.py:35
  99.6 45.2 %collective-permute-start.10 = (bf16[64,8192]{1,0:T(8,128)(2,1)S(1)}, bf16[64,8192]{1,0:T(8,128)(2,1)S(1)}, u32[]{:S(2)}, u32[]{:S(2)}) collective-permute-start(bf16[64,8192]{1,0:T(8,128)(2,1)S(1)} %collective-permute-done.7.refs_0_), channel_id=1, source_target_pairs={{0,32},{32,0},{1,33},{33,1},{2,34},{34,2},{3,35},{35,3},{4,36},{36... | collective-permute-start | bytes 3145736 | tf_op jit(solution)/shard_map/ppermute | solution.py:39
  101.3 43.6 %collective-permute-start.11 = (bf16[64,8192]{1,0:T(8,128)(2,1)}, bf16[64,8192]{1,0:T(8,128)(2,1)S(1)}, u32[]{:S(2)}, u32[]{:S(2)}) collective-permute-start(bf16[64,8192]{1,0:T(8,128)(2,1)} %collective-permute-done.9.refs_1_), channel_id=1, source_target_pairs={{0,32},{32,0},{1,33},{33,1},{2,34},{34,2},{3,35},{35,3},{4,36},{36... | collective-permute-start | bytes 3145736 | tf_op jit(solution)/shard_map/ppermute | solution.py:39
  103.1 3.4 %copy-start.1 = (bf16[8192,512]{1,0:T(8,128)(2,1)S(1)}, bf16[8192,512]{1,0:T(8,128)(2,1)}, u32[]{:S(2)}) copy-start(bf16[8192,512]{1,0:T(8,128)(2,1)} %get-tuple-element.10.refs_3_.refs_5_) | copy-start | bytes 25165828
  106.4 3.4 %copy-start.3 = (bf16[8192,512]{1,0:T(8,128)(2,1)S(1)}, bf16[8192,512]{1,0:T(8,128)(2,1)}, u32[]{:S(2)}) copy-start(bf16[8192,512]{1,0:T(8,128)(2,1)} %get-tuple-element.11.refs_2_.refs_4_) | copy-start | bytes 25165828
  109.8 0.9 copy-start.5
  110.7 0.7 copy-start.6
  111.4 0.7 copy-start.8
  112.1 8.8 %copy-start.7 = (f32[1,512]{1,0:T(1,128)S(1)}, f32[1,512]{1,0:T(1,128)}, u32[]{:S(2)}) copy-start(f32[1,512]{1,0:T(1,128)} %convert_element_type.27.refs_4_.refs_6_) | copy-start | bytes 6148
  120.8 3.4 %copy-start.2 = (bf16[8192,512]{1,0:T(8,128)(2,1)S(1)}, bf16[8192,512]{1,0:T(8,128)(2,1)}, u32[]{:S(2)}) copy-start(bf16[8192,512]{1,0:T(8,128)(2,1)} %get-tuple-element.10.refs_3_.refs_5_) | copy-start | bytes 25165828
  124.2 3.4 %copy-start.4 = (bf16[8192,512]{1,0:T(8,128)(2,1)S(1)}, bf16[8192,512]{1,0:T(8,128)(2,1)}, u32[]{:S(2)}) copy-start(bf16[8192,512]{1,0:T(8,128)(2,1)} %get-tuple-element.11.refs_2_.refs_4_) | copy-start | bytes 25165828
  144.8 27.0 %copy-start.14 = (s32[4]{0:T(128)S(1)}, s32[4]{0:T(128)}, u32[]{:S(2)}) copy-start(s32[4]{0:T(128)} %get-tuple-element.20) | copy-start | bytes 52
  144.8 27.0 %copy-start.15 = (s32[4]{0:T(128)S(1)}, s32[4]{0:T(128)}, u32[]{:S(2)}) copy-start(s32[4]{0:T(128)} %get-tuple-element.21) | copy-start | bytes 52
  153.7 17.5 %all-to-all-start = ((f32[128,1,128]{2,1,0:T(1,128)}), f32[128,1,128]{2,1,0:T(1,128)S(1)}, u32[]{:S(2)}, u32[]{:S(2)}) async-start(f32[128,1,128]{2,1,0:T(1,128)} %bitcast.33), calls=%async_computation | async-start | bytes 131072 | tf_op jit(solution)/shard_map/all_to_all | solution.py:145

commit v2 on v1

v2 whole, which is shorter than its diff:
```python
import functools

import jax
import jax.numpy as jnp
from jax import lax
from jax.experimental import pallas as pl
from jax.experimental.pallas import tpu as pltpu
from jax.sharding import Mesh, PartitionSpec as P

epsilon = 1e-06
ALL = ("xh", "core", "xl", "z", "y")
ORDER = (("y", "x", "z"), ("x", "z", "y"))
ROWS = 256
FOLD = 1024
SCOPED = 12 * 1024 * 1024


def flat_index(x, y, z, core):
    return (x // 2) * 64 + core * 32 + (x % 2) * 16 + z * 4 + y


def shift_pairs(phase, step):
    pairs = []
    for core in range(2):
        at = "xyz".index(ORDER[core][phase])
        for x in range(4):
            for y in range(4):
                for z in range(4):
                    to = [x, y, z]
                    to[at] = (to[at] + step) % 4
                    pairs.append((flat_index(x, y, z, core), flat_index(*to, core)))
    return pairs


def shift(block, phase, step):
    return lax.ppermute(block, ALL, shift_pairs(phase, step))


def sibling(block):
    return lax.ppermute(block, "core", [(0, 1), (1, 0)])


def fold_kernel(gate_ref, up_ref, gain_ref, code_ref, out_ref, spread_ref, sems):
    features, width = gate_ref.shape
    for block in range(features // FOLD):
        at = pl.ds(block * FOLD, FOLD)
        for half, ref in enumerate((gate_ref, up_ref)):
            pltpu.make_async_copy(ref.at[at, :], out_ref.at[half, at, :], sems.at[half, block]).start()

    for row in range(code_ref.shape[0]):
        code = jnp.broadcast_to(code_ref[row : row + 1, :].astype(jnp.float32), (128, 128))
        spread_ref[row * 128 : row * 128 + 128, :] = jnp.transpose(code, (1, 0)).astype(jnp.int32)

    @pl.loop(0, features // FOLD)
    def _(block):
        for half, ref in enumerate((gate_ref, up_ref)):
            at = pl.ds(pl.multiple_of(block * FOLD, FOLD), FOLD)
            pltpu.make_async_copy(ref.at[at, :], out_ref.at[half, at, :], sems.at[half, block]).wait()
        for part in range(FOLD // 128):
            at = pl.multiple_of(block * FOLD + part * 128, 128)
            gain = jnp.transpose(jnp.broadcast_to(gain_ref[:, pl.ds(at, 128)], (128, 128)), (1, 0))
            gain = jnp.concatenate([gain] * (width // 128), axis=1)
            for half in range(2):
                value = out_ref[half, pl.ds(at, 128), :].astype(jnp.float32)
                out_ref[half, pl.ds(at, 128), :] = (value * gain).astype(jnp.bfloat16)


def fold(gate, up, gain, code):
    features, width = gate.shape
    gate, up = (pltpu.with_memory_space_constraint(half, pltpu.HBM) for half in (gate, up))
    return pl.pallas_call(
        fold_kernel,
        out_shape=(pltpu.VMEM((2, features, width), jnp.bfloat16), pltpu.VMEM((code.size, 128), jnp.int32)),
        in_specs=[pl.BlockSpec(memory_space=pltpu.HBM)] * 2 + [pl.BlockSpec(memory_space=pltpu.VMEM)] * 2,
        out_specs=(pl.BlockSpec(memory_space=pltpu.VMEM),) * 2,
        scratch_shapes=[pltpu.SemaphoreType.DMA((2, features // FOLD))],
        compiler_params=pltpu.CompilerParams(vmem_limit_bytes=SCOPED),
        cost_estimate=pl.CostEstimate(flops=2 * features * width, bytes_accessed=4 * features * width, transcendentals=0),
    )(gate, up, gain, code)


def stage_kernel(number, pieces, *refs):
    rows = refs[:pieces]
    weight_ref, head_ref, code_ref, unit_ref, before_ref, out_ref, block_ref = refs[pieces:]
    features = block_ref.shape[1]
    first, squares = 0, []
    for ref in rows:
        count = ref.shape[0]
        for at in range(0, count, 64):
            total = jnp.zeros((64, 128), jnp.float32)
            for lane in range(0, features, 128):
                part = ref[at : at + 64, lane : lane + 128]
                block_ref[first + at : first + at + 64, lane : lane + 128] = part
                part = part.astype(jnp.float32)
                total = total + part * part
            squares.append(jnp.sum(total, axis=1, keepdims=True))
        first += count
    inv_rms = lax.rsqrt(jnp.concatenate(squares, axis=0) / features + epsilon)

    gate = jnp.dot(block_ref[...], weight_ref[0], preferred_element_type=jnp.float32) * inv_rms
    up = jnp.dot(block_ref[...], weight_ref[1], preferred_element_type=jnp.float32) * inv_rms
    activated = gate / (1.0 + jnp.exp(-gate)) * up
    score = jnp.sum(activated * head_ref[...], axis=1, keepdims=True)

    units = ROWS // 8
    code = jnp.concatenate(
        [code_ref[pl.ds(pl.multiple_of(unit_ref[number * units + at] * 8, 8), 8), :] for at in range(units)], axis=0
    )
    owner, pack = code // 1024, code % 1024
    section = unit_ref[128]
    lane = lax.broadcasted_iota(jnp.int32, (ROWS, 128), 1)
    line = jnp.concatenate([owner // 8 == lane, pack // 32 + 32 * section == lane], axis=0)
    line = jnp.where(line, 1.0, 0.0).astype(jnp.bfloat16)
    slot = jnp.concatenate(
        [jnp.where(owner % 8 == lane, score, 0.0), jnp.where(pack % 32 + 8 == lane, score, 0.0)], axis=0
    )
    terms = []
    for _ in range(3):
        terms.append(slot.astype(jnp.bfloat16))
        slot = slot - terms[-1].astype(jnp.float32)
    placed = lax.dot_general(
        line, jnp.concatenate(terms, axis=1), (((0,), (0,)), ((), ())), preferred_element_type=jnp.float32
    )
    out_ref[...] = before_ref[...] + placed[:, 0:128] + placed[:, 128:256] + placed[:, 256:384]


def stage(number, rows, weight, head, code, unit, before):
    _, features, width = weight.shape
    vmem = pl.BlockSpec(memory_space=pltpu.VMEM)
    rows = [pltpu.with_memory_space_constraint(piece, pltpu.VMEM) for piece in rows]
    weight = pltpu.with_memory_space_constraint(weight, pltpu.VMEM)
    code = pltpu.with_memory_space_constraint(code, pltpu.VMEM)
    return pl.pallas_call(
        functools.partial(stage_kernel, number, len(rows)),
        out_shape=jax.ShapeDtypeStruct((128, 128), jnp.float32),
        in_specs=[vmem] * (len(rows) + 3) + [pl.BlockSpec(memory_space=pltpu.SMEM), vmem],
        out_specs=vmem,
        scratch_shapes=[pltpu.VMEM((ROWS, features), jnp.bfloat16)],
        compiler_params=pltpu.CompilerParams(vmem_limit_bytes=SCOPED),
        cost_estimate=pl.CostEstimate(flops=4 * ROWS * features * width, bytes_accessed=4 * features * width, transcendentals=ROWS * width),
    )(*rows, weight, head, code, unit, before)


def unit_table(core, section):
    place = {"x": lax.axis_index("xh") * 2 + lax.axis_index("xl"), "y": lax.axis_index("y"), "z": lax.axis_index("z")}
    at = jnp.arange(128, dtype=jnp.int32)
    number = at // 32
    third = jnp.where(number < 2, number, 5 - number)
    back = (at % 4, at // 4 % 4, third)
    half = jnp.where(at // 16 % 2 == 0, core, 1 - core)
    device = []
    for kind in range(2):
        source = {axis: (place[axis] - back[phase]) % 4 for phase, axis in enumerate(ORDER[kind])}
        device.append(flat_index(source["x"], source["y"], source["z"], kind))
    table = jnp.where(half == 0, device[0], device[1])
    return jnp.concatenate([table, jnp.broadcast_to(section, (128,)).astype(jnp.int32)])


def finish_kernel(arrived_ref, unit_ref, scores_ref, joined_ref):
    def log_sigmoid(value):
        return jnp.minimum(value, 0.0) - jnp.log1p(jnp.exp(-jnp.abs(value)))

    sums = jnp.concatenate(
        [jnp.sum(arrived_ref[at : at + 32, :], axis=0, keepdims=True) for at in range(0, 128, 32)], axis=0
    )
    flipped = lax.broadcasted_iota(jnp.int32, sums.shape, 0) % 2 == 1
    joined_ref[...] = jnp.where(flipped, log_sigmoid(sums), sums)[:, 0:8]
    scores = jnp.sum(sums, axis=0, keepdims=True)
    scores_ref[...] = jnp.where(unit_ref[128] % 2 == 1, log_sigmoid(scores), scores)[:, 8:40]


def finish(arrived, unit):
    vmem = pl.BlockSpec(memory_space=pltpu.VMEM)
    return pl.pallas_call(
        finish_kernel,
        out_shape=(jax.ShapeDtypeStruct((1, 32), jnp.float32), jax.ShapeDtypeStruct((4, 8), jnp.float32)),
        in_specs=[vmem, pl.BlockSpec(memory_space=pltpu.SMEM)],
        out_specs=(vmem, vmem),
        compiler_params=pltpu.CompilerParams(vmem_limit_bytes=SCOPED),
    )(arrived, unit)


def exchange(sent):
    return lax.all_to_all(sent[:, None, :], ALL, split_axis=0, concat_axis=0, tiled=True).reshape(128, 128)


def body(hidden, norm_gain, gate_weight, up_weight, head_vector, pack_slot, owner_slot):
    core = lax.axis_index("core")
    section = lax.axis_index("xh") * 2 + core
    head = head_vector.astype(jnp.float32)
    own_pack = lax.dynamic_index_in_dim(pack_slot, section, 0, keepdims=False)
    code = (owner_slot * 1024 + own_pack).reshape(8, 128)
    unit = unit_table(core, section)
    sent = jnp.zeros((128, 128), jnp.float32)

    line = jnp.concatenate([hidden] + [shift(hidden, 0, step) for step in (1, 2, 3)], axis=0)
    line, gate, up, code, unit, head, sent = lax.optimization_barrier(
        (line, gate_weight[0], up_weight[0], code, unit, head, sent)
    )
    plane = jnp.concatenate([line] + [shift(line, 1, step) for step in (1, 2, 3)], axis=0)
    weight, code = fold(gate, up, norm_gain, code)
    plane, weight, code = lax.optimization_barrier((plane, weight, code))
    other = sibling(plane)
    behind = shift(plane, 2, 1)
    ahead = shift(plane, 2, 3)
    sent, _ = lax.optimization_barrier((sent, plane))
    sent = exchange(sent)
    sent = stage(0, (plane, other), weight, head, code, unit, sent)
    behind, ahead, sent = lax.optimization_barrier((behind, ahead, sent))
    other_behind, other_ahead = sibling(behind), sibling(ahead)
    far_low = shift(behind[:64], 2, 1)
    far_high = shift(ahead[64:], 2, 3)
    sent = stage(1, (behind, other_behind), weight, head, code, unit, sent)
    sent = stage(2, (ahead, other_ahead), weight, head, code, unit, sent)
    far_low, far_high, sent = lax.optimization_barrier((far_low, far_high, sent))
    far = (far_low, far_high, sibling(far_low), sibling(far_high))
    sent = stage(3, far, weight, head, code, unit, sent)

    return finish(exchange(sent), unit)


def solution(mesh):
    parts = Mesh(mesh.devices.reshape(2, 2, 2, 4, 4), ALL)
    section, shard = ("xh", "core"), ("xl", "z", "y")
    in_specs = (
        P(section + shard, None),
        P(section, None),
        P(section, None, shard),
        P(section, None, shard),
        P(section, shard),
        P(),
        P(),
    )
    out_specs = (P(section, shard), P(None, section + shard))
    return jax.shard_map(body, mesh=parts, in_specs=in_specs, out_specs=out_specs, check_vma=False)
```

time: 173 us -> 112 us (0.65)
  blocking collectives: 0 us -> 43.9 us
  local copies, waits for them, and re-layouts: 38 us -> 0.92 us
  waiting for transfers between devices: 42.8 us -> 13.2 us
  other arithmetic: 21.3 us -> 2.53 us
  starting transfers between devices: 34.5 us -> 19.5 us
  Pallas kernels: 34.8 us -> 30.8 us
    all_to_all x0 -> x2, blocking collectives: none -> 43.9 us  [exchange(): lax.all_to_all(sent[:, None, :], ALL, split_axis=0, concat_axis=0, tiled=...]
    ppermute x10, waiting for transfers between devices: 33.3 us -> 8.03 us  [shift(): return lax.ppermute(block, ALL, shift_pairs(phase, step))]
    unnamed x37 -> x4, local copies, waits for them, and re-layouts: 20.4 us -> 0.77 us
    convert_element_type x1 -> x0, other arithmetic: 12.3 us -> none  [body(): up = (up_weight[0].astype(jnp.float32) * gain).astype(jnp.bfloat16)]
    gather x8 -> x0, local copies, waits for them, and re-layouts: 10.9 us -> none  [body(): owner, pack = (owner_slot[token], own_pack[token])]
    all_to_all x1 -> x0, waiting for transfers between devices: 9.49 us -> none  [body(): lax.all_to_all(sent[:, None, :], ALL, split_axis=0, concat_axis=0, tiled=...]
    all_to_all x1 -> x0, starting transfers between devices: 7.96 us -> none  [body(): lax.all_to_all(sent[:, None, :], ALL, split_axis=0, concat_axis=0, tiled=...]
    ppermute x5, starting transfers between devices: 9.71 us -> 3.33 us  [sibling(): return lax.ppermute(block, 'core', [(0, 1), (1, 0)])]
  transfers between devices with their start and end apart: 16 -> 15, of which waited for: 7 -> 7; matrix products, arithmetic and copies ran while one was open for 24% -> 1% of each run, Pallas kernels for 15% -> 21%
where the time goes in v2:
time: 112 us
  blocking collectives  43.9 us (39%)
  Pallas kernels  30.8 us (28%)
  starting transfers between devices  19.5 us (17%)
  waiting for transfers between devices  13.2 us (12%)
  other arithmetic  2.53 us (2%)
    all_to_all x2, blocking collectives, exchange(): lax.all_to_all(sent[:, None, :], ALL, split_axis=0, concat_axis=0, tiled=...  43.9 us
    pallas_call x4, Pallas kernels, stage(): pl.pallas_call(functools.partial(stage_kernel, number, len(rows)), out_sh...  23.2 us
    ppermute x10, starting transfers between devices, shift(): return lax.ppermute(block, ALL, shift_pairs(phase, step))  16.1 us
    ppermute x10, waiting for transfers between devices, shift(): return lax.ppermute(block, ALL, shift_pairs(phase, step))  8.03 us
    pallas_call x1, Pallas kernels, fold(): pl.pallas_call(fold_kernel, out_shape=(pltpu.VMEM((2, features, width), j...  6.38 us
    ppermute x5, waiting for transfers between devices, sibling(): return lax.ppermute(block, 'core', [(0, 1), (1, 0)])  5.18 us
    ppermute x5, starting transfers between devices, sibling(): return lax.ppermute(block, 'core', [(0, 1), (1, 0)])  3.33 us
  transfers between devices with their start and end apart: 15, of which 7 were waited for; matrix products, arithmetic and copies ran while one was open for 1% of the time, Pallas kernels for 21%

profile of v2, /device:TPU:1, one launch (start us, length us, event | category | flops | bytes accessed | tf_op | source)
XLA Modules:
  0.0 111.5 jit_solution(15110391907532792410)
XLA Ops:
  0.6 0.0 copy-start
  0.6 2.1 %collective-permute-start = (bf16[8,8192]{1,0:T(8,128)(2,1)}, bf16[8,8192]{1,0:T(8,128)(2,1)S(1)}, u32[]{:S(2)}, u32[]{:S(2)}) collective-permute-start(bf16[8,8192]{1,0:T(8,128)(2,1)} %param.7), channel_id=1, source_target_pairs={{0,1},{4,5},{8,9},{12,13},{1,2},{5,6},{9,10},{13,14},{2,3},{6,7},{... | collective-permute-start | bytes 393224 | tf_op jit(solution)/shard_map/ppermute | solution.py:36
  2.8 2.5 %collective-permute-start.1 = (bf16[8,8192]{1,0:T(8,128)(2,1)}, bf16[8,8192]{1,0:T(8,128)(2,1)S(1)}, u32[]{:S(2)}, u32[]{:S(2)}) collective-permute-start(bf16[8,8192]{1,0:T(8,128)(2,1)} %param.7), channel_id=1, source_target_pairs={{0,2},{4,6},{8,10},{12,14},{1,3},{5,7},{9,11},{13,15},{2,0},{6,4},... | collective-permute-start | bytes 393224 | tf_op jit(solution)/shard_map/ppermute | solution.py:36
  5.2 1.2 %collective-permute-start.2 = (bf16[8,8192]{1,0:T(8,128)(2,1)}, bf16[8,8192]{1,0:T(8,128)(2,1)S(1)}, u32[]{:S(2)}, u32[]{:S(2)}) collective-permute-start(bf16[8,8192]{1,0:T(8,128)(2,1)} %param.7), channel_id=1, source_target_pairs={{0,3},{4,7},{8,11},{12,15},{1,0},{5,4},{9,8},{13,12},{2,1},{6,5},{... | collective-permute-start | bytes 393224 | tf_op jit(solution)/shard_map/ppermute | solution.py:36
  6.4 0.7 convert_element_type.3.refs_3_.refs_5_
  7.1 0.0 copy-done
  7.1 0.7 add_bitcast_fusion.code_ref
  7.8 0.0 collective-permute-done
  7.8 1.7 %collective-permute-done.1 = bf16[8,8192]{1,0:T(8,128)(2,1)S(1)} collective-permute-done((bf16[8,8192]{1,0:T(8,128)(2,1)}, bf16[8,8192]{1,0:T(8,128)(2,1)S(1)}, u32[]{:S(2)}, u32[]{:S(2)}) %collective-permute-start.1) | collective-permute-done | bytes 131104 | tf_op jit(solution)/shard_map/ppermute | solution.py:36
  9.5 0.1 collective-permute-done.2
  9.5 0.9 pad_maximum_fusion.1
  10.5 1.7 %collective-permute-start.3 = (bf16[32,8192]{1,0:T(8,128)(2,1)S(1)}, bf16[32,8192]{1,0:T(8,128)(2,1)S(1)}, u32[]{:S(2)}, u32[]{:S(2)}) collective-permute-start(bf16[32,8192]{1,0:T(8,128)(2,1)S(1)} %pad_maximum_fusion.1), channel_id=1, source_target_pairs={{0,16},{4,20},{8,24},{12,28},{1,17},{5,21},{9,25},{13,29},{2,18},{... | collective-permute-start | bytes 1572872 | tf_op jit(solution)/shard_map/ppermute | solution.py:36
  12.2 3.3 %collective-permute-start.4 = (bf16[32,8192]{1,0:T(8,128)(2,1)S(1)}, bf16[32,8192]{1,0:T(8,128)(2,1)S(1)}, u32[]{:S(2)}, u32[]{:S(2)}) collective-permute-start(bf16[32,8192]{1,0:T(8,128)(2,1)S(1)} %pad_maximum_fusion.1), channel_id=1, source_target_pairs={{0,64},{4,68},{8,72},{12,76},{1,65},{5,69},{9,73},{13,77},{2,66},{... | collective-permute-start | bytes 1572872 | tf_op jit(solution)/shard_map/ppermute | solution.py:36
  15.5 0.7 collective-permute-start.5
  16.2 0.0 copy-start.1
  16.2 0.8 copy-done.1
  17.0 6.4 %shard_map.86 = (bf16[2,8192,512]{2,1,0:T(8,128)(2,1)S(1)}, s32[1024,128]{1,0:T(8,128)S(1)}) custom-call(bf16[8192,512]{1,0:T(8,128)(2,1)} %bitcast.14, bf16[8192,512]{1,0:T(8,128)(2,1)} %bitcast.15, f32[1,8192]{1,0:T(1,128)S(1)} %copy-done.1, s32[8,128]{1,0:T(8,128)S(1)} %add_bitcast_fusion.code_ref), custom_call_target="tpu_custom_call" | custom-call | flops 8388608 | bytes 16777216 | tf_op jit(solution)/shard_map/pallas_call | solution.py:71
  23.4 0.0 collective-permute-done.3
  23.4 4.6 %collective-permute-done.4 = bf16[32,8192]{1,0:T(8,128)(2,1)S(1)} collective-permute-done((bf16[32,8192]{1,0:T(8,128)(2,1)S(1)}, bf16[32,8192]{1,0:T(8,128)(2,1)S(1)}, u32[]{:S(2)}, u32[]{:S(2)}) %collective-permute-start.4) | collective-permute-done | bytes 524320 | tf_op jit(solution)/shard_map/ppermute | solution.py:36
  28.0 0.0 collective-permute-done.5
  28.0 0.2 pad_maximum_fusion.refs_0_
  28.1 2.0 %collective-permute-start.8 = (bf16[128,8192]{1,0:T(8,128)(2,1)S(1)}, bf16[128,8192]{1,0:T(8,128)(2,1)S(1)}, u32[]{:S(2)}, u32[]{:S(2)}) collective-permute-start(bf16[128,8192]{1,0:T(8,128)(2,1)S(1)} %pad_maximum_fusion.refs_0_), channel_id=1, source_target_pairs={{0,32},{32,0},{1,33},{33,1},{2,34},{34,2},{3,35},{35,3},{4,36},{36... | collective-permute-start | bytes 6291464 | tf_op jit(solution)/shard_map/ppermute | solution.py:40
  30.2 0.7 collective-permute-start.6
  30.9 1.9 %collective-permute-start.7 = (bf16[128,8192]{1,0:T(8,128)(2,1)S(1)}, bf16[128,8192]{1,0:T(8,128)(2,1)S(1)}, u32[]{:S(2)}, u32[]{:S(2)}) collective-permute-start(bf16[128,8192]{1,0:T(8,128)(2,1)S(1)} %pad_maximum_fusion.refs_0_), channel_id=1, source_target_pairs={{0,12},{4,0},{8,4},{12,8},{1,13},{5,1},{9,5},{13,9},{2,14},{6,2},{... | collective-permute-start | bytes 6291464 | tf_op jit(solution)/shard_map/ppermute | solution.py:36
  32.8 28.3 %all_to_all.10 = f32[128,1,128]{2,1,0:T(1,128)S(1)} all-to-all(f32[128,1,128]{2,1,0:T(1,128)S(1)} %bitcast.16), channel_id=1, replica_groups=mesh['xh'=2,'core'=2,'xl'=2,'z'=4,'y'=4] {'xh','core','xl','z','y'}, dimensions={0} | all-to-all | bytes 131072 | tf_op jit(solution)/shard_map/all_to_all | solution.py:184
  61.2 0.0 collective-permute-done.8.refs_1_
  61.2 5.8 %shard_map.87.refs_6_ = f32[128,128]{1,0:T(8,128)S(1)} custom-call(bf16[128,8192]{1,0:T(8,128)(2,1)S(1)} %pad_maximum_fusion.refs_0_, bf16[128,8192]{1,0:T(8,128)(2,1)S(1)} %collective-permute-done.8.refs_1_, bf16[2,8192,512]{2,1,0:T(8,128)(2,1)S(1)} %get-tuple-element.28.refs_2_.refs_4_, f32[1,512]{1,0:T(1,128)S(1)} %convert_element_type.3.refs_3_.refs_5_, ...), custom_call_target="tpu_custom_call" | custom-call | flops 4294967296 | bytes 16777216 | tf_op jit(solution)/shard_map/pallas_call | solution.py:133
  67.0 0.0 collective-permute-done.6.refs_0_
  67.0 0.0 collective-permute-done.7.refs_0_
  67.0 0.7 collective-permute-start.12
  67.7 0.1 collective-permute-start.11
  67.8 0.1 slice.7
  67.9 0.1 slice.6
  68.0 2.0 %collective-permute-start.10 = (bf16[64,8192]{1,0:T(8,128)(2,1)S(1)}, bf16[64,8192]{1,0:T(8,128)(2,1)S(1)}, u32[]{:S(2)}, u32[]{:S(2)}) collective-permute-start(bf16[64,8192]{1,0:T(8,128)(2,1)S(1)} %slice.7), channel_id=1, source_target_pairs={{0,12},{4,0},{8,4},{12,8},{1,13},{5,1},{9,5},{13,9},{2,14},{6,2},{... | collective-permute-start | bytes 3145736 | tf_op jit(solution)/shard_map/ppermute | solution.py:36
  70.0 0.0 collective-permute-start.9
  70.0 1.5 %collective-permute-done.12.refs_1_ = bf16[128,8192]{1,0:T(8,128)(2,1)S(1)} collective-permute-done((bf16[128,8192]{1,0:T(8,128)(2,1)S(1)}, bf16[128,8192]{1,0:T(8,128)(2,1)S(1)}, u32[]{:S(2)}, u32[]{:S(2)}) %collective-permute-start.12) | collective-permute-done | bytes 2097184 | tf_op jit(solution)/shard_map/ppermute | solution.py:40
  71.5 5.8 %shard_map.88.refs_6_ = f32[128,128]{1,0:T(8,128)S(1)} custom-call(bf16[128,8192]{1,0:T(8,128)(2,1)S(1)} %collective-permute-done.6.refs_0_, bf16[128,8192]{1,0:T(8,128)(2,1)S(1)} %collective-permute-done.12.refs_1_, bf16[2,8192,512]{2,1,0:T(8,128)(2,1)S(1)} %get-tuple-element.28.refs_2_.refs_4_, f32[1,512]{1,0:T(1,128)S(1)} %convert_element_type.3.refs_3_.refs_5_, ...), custom_call_target="tpu_custom_call" | custom-call | flops 4294967296 | bytes 16777216 | tf_op jit(solution)/shard_map/pallas_call | solution.py:133
  77.3 0.0 collective-permute-done.11.refs_1_
  77.3 5.8 %shard_map.89.refs_8_ = f32[128,128]{1,0:T(8,128)S(1)} custom-call(bf16[128,8192]{1,0:T(8,128)(2,1)S(1)} %collective-permute-done.7.refs_0_, bf16[128,8192]{1,0:T(8,128)(2,1)S(1)} %collective-permute-done.11.refs_1_, bf16[2,8192,512]{2,1,0:T(8,128)(2,1)S(1)} %get-tuple-element.28.refs_2_.refs_4_, f32[1,512]{1,0:T(1,128)S(1)} %convert_element_type.3.refs_3_.refs_5_, ...), custom_call_target="tpu_custom_call" | custom-call | flops 4294967296 | bytes 16777216 | tf_op jit(solution)/shard_map/pallas_call | solution.py:133
  83.1 0.0 collective-permute-done.10.refs_1_
  83.1 1.7 %collective-permute-done.9.refs_0_ = bf16[64,8192]{1,0:T(8,128)(2,1)S(1)} collective-permute-done((bf16[64,8192]{1,0:T(8,128)(2,1)S(1)}, bf16[64,8192]{1,0:T(8,128)(2,1)S(1)}, u32[]{:S(2)}, u32[]{:S(2)}) %collective-permute-start.9) | collective-permute-done | bytes 1048608 | tf_op jit(solution)/shard_map/ppermute | solution.py:36
  84.8 0.2 collective-permute-start.13
  85.1 0.3 collective-permute-start.14
  85.3 2.1 %collective-permute-done.13.refs_2_ = bf16[64,8192]{1,0:T(8,128)(2,1)S(1)} collective-permute-done((bf16[64,8192]{1,0:T(8,128)(2,1)S(1)}, bf16[64,8192]{1,0:T(8,128)(2,1)S(1)}, u32[]{:S(2)}, u32[]{:S(2)}) %collective-permute-start.13) | collective-permute-done | bytes 1048608 | tf_op jit(solution)/shard_map/ppermute | solution.py:40
  87.5 1.5 %collective-permute-done.14.refs_3_ = bf16[64,8192]{1,0:T(8,128)(2,1)S(1)} collective-permute-done((bf16[64,8192]{1,0:T(8,128)(2,1)S(1)}, bf16[64,8192]{1,0:T(8,128)(2,1)S(1)}, u32[]{:S(2)}, u32[]{:S(2)}) %collective-permute-start.14) | collective-permute-done | bytes 1048608 | tf_op jit(solution)/shard_map/ppermute | solution.py:40
  89.0 5.8 %shard_map.90 = f32[128,128]{1,0:T(8,128)S(1)} custom-call(bf16[64,8192]{1,0:T(8,128)(2,1)S(1)} %collective-permute-done.9.refs_0_, bf16[64,8192]{1,0:T(8,128)(2,1)S(1)} %collective-permute-done.10.refs_1_, bf16[64,8192]{1,0:T(8,128)(2,1)S(1)} %collective-permute-done.13.refs_2_, bf16[64,8192]{1,0:T(8,128)(2,1)S(1)} %collective-permute-done.14.refs_3_, ...), custom_call_target="tpu_custom_call" | custom-call | flops 4294967296 | bytes 16777216 | tf_op jit(solution)/shard_map/pallas_call | solution.py:133
  94.8 15.6 %all_to_all.11 = f32[128,1,128]{2,1,0:T(1,128)S(1)} all-to-all(f32[128,1,128]{2,1,0:T(1,128)S(1)} %bitcast.11), channel_id=1, replica_groups=mesh['xh'=2,'core'=2,'xl'=2,'z'=4,'y'=4] {'xh','core','xl','z','y'}, dimensions={0} | all-to-all | bytes 131072 | tf_op jit(solution)/shard_map/all_to_all | solution.py:184
  110.4 1.2 %shard_map.91 = (f32[1,32]{1,0:T(1,128)}, f32[4,8]{1,0:T(4,128)}) custom-call(f32[128,128]{1,0:T(8,128)S(1)} %bitcast.13, s32[256]{0:T(256)S(1)} %concatenate.10.refs_5_.refs_7_.unit_ref), custom_call_target="tpu_custom_call" | custom-call | tf_op jit(solution)/shard_map/pallas_call | solution.py:174
  (4 shorter events, 0.0 us)
Async XLA Ops:
  0.6 6.5 %copy-start = (s32[4,1024]{1,0:T(4,128)S(1)}, s32[4,1024]{1,0:T(4,128)}, u32[]{:S(2)}) copy-start(s32[4,1024]{1,0:T(4,128)} %param.12) | copy-start | bytes 49156
  0.6 7.2 %collective-permute-start = (bf16[8,8192]{1,0:T(8,128)(2,1)}, bf16[8,8192]{1,0:T(8,128)(2,1)S(1)}, u32[]{:S(2)}, u32[]{:S(2)}) collective-permute-start(bf16[8,8192]{1,0:T(8,128)(2,1)} %param.7), channel_id=1, source_target_pairs={{0,1},{4,5},{8,9},{12,13},{1,2},{5,6},{9,10},{13,14},{2,3},{6,7},{... | collective-permute-start | bytes 393224 | tf_op jit(solution)/shard_map/ppermute | solution.py:36
  2.8 6.7 %collective-permute-start.1 = (bf16[8,8192]{1,0:T(8,128)(2,1)}, bf16[8,8192]{1,0:T(8,128)(2,1)S(1)}, u32[]{:S(2)}, u32[]{:S(2)}) collective-permute-start(bf16[8,8192]{1,0:T(8,128)(2,1)} %param.7), channel_id=1, source_target_pairs={{0,2},{4,6},{8,10},{12,14},{1,3},{5,7},{9,11},{13,15},{2,0},{6,4},... | collective-permute-start | bytes 393224 | tf_op jit(solution)/shard_map/ppermute | solution.py:36
  5.2 4.3 %collective-permute-start.2 = (bf16[8,8192]{1,0:T(8,128)(2,1)}, bf16[8,8192]{1,0:T(8,128)(2,1)S(1)}, u32[]{:S(2)}, u32[]{:S(2)}) collective-permute-start(bf16[8,8192]{1,0:T(8,128)(2,1)} %param.7), channel_id=1, source_target_pairs={{0,3},{4,7},{8,11},{12,15},{1,0},{5,4},{9,8},{13,12},{2,1},{6,5},{... | collective-permute-start | bytes 393224 | tf_op jit(solution)/shard_map/ppermute | solution.py:36
  10.5 12.9 %collective-permute-start.3 = (bf16[32,8192]{1,0:T(8,128)(2,1)S(1)}, bf16[32,8192]{1,0:T(8,128)(2,1)S(1)}, u32[]{:S(2)}, u32[]{:S(2)}) collective-permute-start(bf16[32,8192]{1,0:T(8,128)(2,1)S(1)} %pad_maximum_fusion.1), channel_id=1, source_target_pairs={{0,16},{4,20},{8,24},{12,28},{1,17},{5,21},{9,25},{13,29},{2,18},{... | collective-permute-start | bytes 1572872 | tf_op jit(solution)/shard_map/ppermute | solution.py:36
  12.2 15.8 %collective-permute-start.4 = (bf16[32,8192]{1,0:T(8,128)(2,1)S(1)}, bf16[32,8192]{1,0:T(8,128)(2,1)S(1)}, u32[]{:S(2)}, u32[]{:S(2)}) collective-permute-start(bf16[32,8192]{1,0:T(8,128)(2,1)S(1)} %pad_maximum_fusion.1), channel_id=1, source_target_pairs={{0,64},{4,68},{8,72},{12,76},{1,65},{5,69},{9,73},{13,77},{2,66},{... | collective-permute-start | bytes 1572872 | tf_op jit(solution)/shard_map/ppermute | solution.py:36
  15.5 12.5 %collective-permute-start.5 = (bf16[32,8192]{1,0:T(8,128)(2,1)S(1)}, bf16[32,8192]{1,0:T(8,128)(2,1)S(1)}, u32[]{:S(2)}, u32[]{:S(2)}) collective-permute-start(bf16[32,8192]{1,0:T(8,128)(2,1)S(1)} %pad_maximum_fusion.1), channel_id=1, source_target_pairs={{0,80},{4,84},{8,88},{12,92},{1,81},{5,85},{9,89},{13,93},{2,82},{... | collective-permute-start | bytes 1572872 | tf_op jit(solution)/shard_map/ppermute | solution.py:36
  16.2 0.8 copy-start.1
  28.1 33.0 %collective-permute-start.8 = (bf16[128,8192]{1,0:T(8,128)(2,1)S(1)}, bf16[128,8192]{1,0:T(8,128)(2,1)S(1)}, u32[]{:S(2)}, u32[]{:S(2)}) collective-permute-start(bf16[128,8192]{1,0:T(8,128)(2,1)S(1)} %pad_maximum_fusion.refs_0_), channel_id=1, source_target_pairs={{0,32},{32,0},{1,33},{33,1},{2,34},{34,2},{3,35},{35,3},{4,36},{36... | collective-permute-start | bytes 6291464 | tf_op jit(solution)/shard_map/ppermute | solution.py:40
  30.2 36.8 %collective-permute-start.6 = (bf16[128,8192]{1,0:T(8,128)(2,1)S(1)}, bf16[128,8192]{1,0:T(8,128)(2,1)S(1)}, u32[]{:S(2)}, u32[]{:S(2)}) collective-permute-start(bf16[128,8192]{1,0:T(8,128)(2,1)S(1)} %pad_maximum_fusion.refs_0_), channel_id=1, source_target_pairs={{0,4},{4,8},{8,12},{12,0},{1,5},{5,9},{9,13},{13,1},{2,6},{6,10},{... | collective-permute-start | bytes 6291464 | tf_op jit(solution)/shard_map/ppermute | solution.py:36
  30.9 36.1 %collective-permute-start.7 = (bf16[128,8192]{1,0:T(8,128)(2,1)S(1)}, bf16[128,8192]{1,0:T(8,128)(2,1)S(1)}, u32[]{:S(2)}, u32[]{:S(2)}) collective-permute-start(bf16[128,8192]{1,0:T(8,128)(2,1)S(1)} %pad_maximum_fusion.refs_0_), channel_id=1, source_target_pairs={{0,12},{4,0},{8,4},{12,8},{1,13},{5,1},{9,5},{13,9},{2,14},{6,2},{... | collective-permute-start | bytes 6291464 | tf_op jit(solution)/shard_map/ppermute | solution.py:36
  67.0 4.5 %collective-permute-start.12 = (bf16[128,8192]{1,0:T(8,128)(2,1)S(1)}, bf16[128,8192]{1,0:T(8,128)(2,1)S(1)}, u32[]{:S(2)}, u32[]{:S(2)}) collective-permute-start(bf16[128,8192]{1,0:T(8,128)(2,1)S(1)} %collective-permute-done.6.refs_0_), channel_id=1, source_target_pairs={{0,32},{32,0},{1,33},{33,1},{2,34},{34,2},{3,35},{35,3},{4,36},{36... | collective-permute-start | bytes 6291464 | tf_op jit(solution)/shard_map/ppermute | solution.py:40
  67.7 9.6 %collective-permute-start.11 = (bf16[128,8192]{1,0:T(8,128)(2,1)S(1)}, bf16[128,8192]{1,0:T(8,128)(2,1)S(1)}, u32[]{:S(2)}, u32[]{:S(2)}) collective-permute-start(bf16[128,8192]{1,0:T(8,128)(2,1)S(1)} %collective-permute-done.7.refs_0_), channel_id=1, source_target_pairs={{0,32},{32,0},{1,33},{33,1},{2,34},{34,2},{3,35},{35,3},{4,36},{36... | collective-permute-start | bytes 6291464 | tf_op jit(solution)/shard_map/ppermute | solution.py:40
  68.0 15.2 %collective-permute-start.10 = (bf16[64,8192]{1,0:T(8,128)(2,1)S(1)}, bf16[64,8192]{1,0:T(8,128)(2,1)S(1)}, u32[]{:S(2)}, u32[]{:S(2)}) collective-permute-start(bf16[64,8192]{1,0:T(8,128)(2,1)S(1)} %slice.7), channel_id=1, source_target_pairs={{0,12},{4,0},{8,4},{12,8},{1,13},{5,1},{9,5},{13,9},{2,14},{6,2},{... | collective-permute-start | bytes 3145736 | tf_op jit(solution)/shard_map/ppermute | solution.py:36
  70.0 14.9 %collective-permute-start.9 = (bf16[64,8192]{1,0:T(8,128)(2,1)S(1)}, bf16[64,8192]{1,0:T(8,128)(2,1)S(1)}, u32[]{:S(2)}, u32[]{:S(2)}) collective-permute-start(bf16[64,8192]{1,0:T(8,128)(2,1)S(1)} %slice.6), channel_id=1, source_target_pairs={{0,4},{4,8},{8,12},{12,0},{1,5},{5,9},{9,13},{13,1},{2,6},{6,10},{... | collective-permute-start | bytes 3145736 | tf_op jit(solution)/shard_map/ppermute | solution.py:36
  84.8 2.7 %collective-permute-start.13 = (bf16[64,8192]{1,0:T(8,128)(2,1)S(1)}, bf16[64,8192]{1,0:T(8,128)(2,1)S(1)}, u32[]{:S(2)}, u32[]{:S(2)}) collective-permute-start(bf16[64,8192]{1,0:T(8,128)(2,1)S(1)} %collective-permute-done.9.refs_0_), channel_id=1, source_target_pairs={{0,32},{32,0},{1,33},{33,1},{2,34},{34,2},{3,35},{35,3},{4,36},{36... | collective-permute-start | bytes 3145736 | tf_op jit(solution)/shard_map/ppermute | solution.py:40
  85.1 3.9 %collective-permute-start.14 = (bf16[64,8192]{1,0:T(8,128)(2,1)S(1)}, bf16[64,8192]{1,0:T(8,128)(2,1)S(1)}, u32[]{:S(2)}, u32[]{:S(2)}) collective-permute-start(bf16[64,8192]{1,0:T(8,128)(2,1)S(1)} %collective-permute-done.10.refs_1_), channel_id=1, source_target_pairs={{0,32},{32,0},{1,33},{33,1},{2,34},{34,2},{3,35},{35,3},{4,36},{36... | collective-permute-start | bytes 3145736 | tf_op jit(solution)/shard_map/ppermute | solution.py:40

commit v3 on v2

--- a/solution.py
+++ b/solution.py
@@ -10,7 +10,6 @@
 epsilon = 1e-06
 ALL = ("xh", "core", "xl", "z", "y")
 ORDER = (("y", "x", "z"), ("x", "z", "y"))
-ROWS = 256
 FOLD = 1024
 SCOPED = 12 * 1024 * 1024
 
@@ -79,7 +78,7 @@
     )(gate, up, gain, code)
 
 
-def stage_kernel(number, pieces, *refs):
+def stage_kernel(units, pieces, *refs):
     rows = refs[:pieces]
     weight_ref, head_ref, code_ref, unit_ref, before_ref, out_ref, block_ref = refs[pieces:]
     features = block_ref.shape[1]
@@ -102,13 +101,11 @@
     activated = gate / (1.0 + jnp.exp(-gate)) * up
     score = jnp.sum(activated * head_ref[...], axis=1, keepdims=True)
 
-    units = ROWS // 8
-    code = jnp.concatenate(
-        [code_ref[pl.ds(pl.multiple_of(unit_ref[number * units + at] * 8, 8), 8), :] for at in range(units)], axis=0
-    )
+    rows = 8 * len(units)
+    code = jnp.concatenate([code_ref[pl.ds(pl.multiple_of(unit_ref[at] * 8, 8), 8), :] for at in units], axis=0)
     owner, pack = code // 1024, code % 1024
     section = unit_ref[128]
-    lane = lax.broadcasted_iota(jnp.int32, (ROWS, 128), 1)
+    lane = lax.broadcasted_iota(jnp.int32, (rows, 128), 1)
     line = jnp.concatenate([owner // 8 == lane, pack // 32 + 32 * section == lane], axis=0)
     line = jnp.where(line, 1.0, 0.0).astype(jnp.bfloat16)
     slot = jnp.concatenate(
@@ -124,29 +121,33 @@
     out_ref[...] = before_ref[...] + placed[:, 0:128] + placed[:, 128:256] + placed[:, 256:384]
 
 
-def stage(number, rows, weight, head, code, unit, before):
+def stage(pieces, weight, head, code, unit, before):
     _, features, width = weight.shape
     vmem = pl.BlockSpec(memory_space=pltpu.VMEM)
-    rows = [pltpu.with_memory_space_constraint(piece, pltpu.VMEM) for piece in rows]
+    arrays = [pltpu.with_memory_space_constraint(piece, pltpu.VMEM) for piece, _ in pieces]
+    units = tuple(at for _, held in pieces for at in held)
+    rows = 8 * len(units)
     weight = pltpu.with_memory_space_constraint(weight, pltpu.VMEM)
     code = pltpu.with_memory_space_constraint(code, pltpu.VMEM)
     return pl.pallas_call(
-        functools.partial(stage_kernel, number, len(rows)),
+        functools.partial(stage_kernel, units, len(arrays)),
         out_shape=jax.ShapeDtypeStruct((128, 128), jnp.float32),
-        in_specs=[vmem] * (len(rows) + 3) + [pl.BlockSpec(memory_space=pltpu.SMEM), vmem],
+        in_specs=[vmem] * (len(arrays) + 3) + [pl.BlockSpec(memory_space=pltpu.SMEM), vmem],
         out_specs=vmem,
-        scratch_shapes=[pltpu.VMEM((ROWS, features), jnp.bfloat16)],
+        scratch_shapes=[pltpu.VMEM((rows, features), jnp.bfloat16)],
         compiler_params=pltpu.CompilerParams(vmem_limit_bytes=SCOPED),
-        cost_estimate=pl.CostEstimate(flops=4 * ROWS * features * width, bytes_accessed=4 * features * width, transcendentals=ROWS * width),
-    )(*rows, weight, head, code, unit, before)
+        cost_estimate=pl.CostEstimate(flops=4 * rows * features * width, bytes_accessed=4 * features * width, transcendentals=rows * width),
+    )(*arrays, weight, head, code, unit, before)
+
+
+def held(half, third, lines):
+    return tuple(third * 32 + half * 16 + line * 4 + at for line in lines for at in range(4))
 
 
 def unit_table(core, section):
     place = {"x": lax.axis_index("xh") * 2 + lax.axis_index("xl"), "y": lax.axis_index("y"), "z": lax.axis_index("z")}
     at = jnp.arange(128, dtype=jnp.int32)
-    number = at // 32
-    third = jnp.where(number < 2, number, 5 - number)
-    back = (at % 4, at // 4 % 4, third)
+    back = (at % 4, at // 4 % 4, at // 32)
     half = jnp.where(at // 16 % 2 == 0, core, 1 - core)
     device = []
     for kind in range(2):
@@ -200,21 +201,21 @@
     plane = jnp.concatenate([line] + [shift(line, 1, step) for step in (1, 2, 3)], axis=0)
     weight, code = fold(gate, up, norm_gain, code)
     plane, weight, code = lax.optimization_barrier((plane, weight, code))
+    rest = (weight, head, code, unit)
+    every = (0, 1, 2, 3)
     other = sibling(plane)
     behind = shift(plane, 2, 1)
     ahead = shift(plane, 2, 3)
-    sent, _ = lax.optimization_barrier((sent, plane))
-    sent = exchange(sent)
-    sent = stage(0, (plane, other), weight, head, code, unit, sent)
+    sent = stage(((plane, held(0, 0, every)), (other, held(1, 0, every))), *rest, sent)
     behind, ahead, sent = lax.optimization_barrier((behind, ahead, sent))
-    other_behind, other_ahead = sibling(behind), sibling(ahead)
     far_low = shift(behind[:64], 2, 1)
     far_high = shift(ahead[64:], 2, 3)
-    sent = stage(1, (behind, other_behind), weight, head, code, unit, sent)
-    sent = stage(2, (ahead, other_ahead), weight, head, code, unit, sent)
+    sent = stage(((behind, held(0, 1, every)), (sibling(behind), held(1, 1, every))), *rest, sent)
+    sent = stage(((ahead, held(0, 3, every)), (sibling(ahead), held(1, 3, every))), *rest, sent)
     far_low, far_high, sent = lax.optimization_barrier((far_low, far_high, sent))
-    far = (far_low, far_high, sibling(far_low), sibling(far_high))
-    sent = stage(3, far, weight, head, code, unit, sent)
+    far = ((sibling(far_low), held(1, 2, (0, 1))), (sibling(far_high), held(1, 2, (2, 3))))
+    sent = stage(((far_low, held(0, 2, (0, 1))), (far_high, held(0, 2, (2, 3)))), *rest, sent)
+    sent = stage(far, *rest, sent)
 
     return finish(exchange(sent), unit)
 

time: 112 us -> 102 us (0.911)
  blocking collectives: 43.9 us -> 15.5 us
  waiting for transfers between devices: 13.2 us -> 28.1 us
  starting transfers between devices: 19.5 us -> 22.6 us
    all_to_all x2 -> x1, blocking collectives: 43.9 us -> 15.5 us  [exchange(): lax.all_to_all(sent[:, None, :], ALL, split_axis=0, concat_axis=0, tiled=...]
    ppermute x10, waiting for transfers between devices: 8.03 us -> 25.3 us  [shift(): return lax.ppermute(block, ALL, shift_pairs(phase, step))]
    ppermute x5, starting transfers between devices: 3.33 us -> 6.14 us  [sibling(): return lax.ppermute(block, 'core', [(0, 1), (1, 0)])]
    ppermute x5, waiting for transfers between devices: 5.18 us -> 2.79 us  [sibling(): return lax.ppermute(block, 'core', [(0, 1), (1, 0)])]
    pallas_call x4 -> x5, Pallas kernels: 23.2 us -> 24.2 us  [stage(): pl.pallas_call(functools.partial(stage_kernel, units, len(arrays)), out_s...]
  transfers between devices with their start and end apart: 15 -> 15, of which waited for: 7 -> 8; matrix products, arithmetic and copies ran while one was open for 1% -> 2% of each run, Pallas kernels for 21% -> 27%
where the time goes in v3:
time: 102 us
  Pallas kernels  31.7 us (31%)
  waiting for transfers between devices  28.1 us (28%)
  starting transfers between devices  22.6 us (22%)
  blocking collectives  15.5 us (15%)
  other arithmetic  2.53 us (2%)
    ppermute x10, waiting for transfers between devices, shift(): return lax.ppermute(block, ALL, shift_pairs(phase, step))  25.3 us
    pallas_call x5, Pallas kernels, stage(): pl.pallas_call(functools.partial(stage_kernel, units, len(arrays)), out_s...  24.2 us
    ppermute x10, starting transfers between devices, shift(): return lax.ppermute(block, ALL, shift_pairs(phase, step))  16.5 us
    all_to_all x1, blocking collectives, exchange(): lax.all_to_all(sent[:, None, :], ALL, split_axis=0, concat_axis=0, tiled=...  15.5 us
    pallas_call x1, Pallas kernels, fold(): pl.pallas_call(fold_kernel, out_shape=(pltpu.VMEM((2, features, width), j...  6.38 us
    ppermute x5, starting transfers between devices, sibling(): return lax.ppermute(block, 'core', [(0, 1), (1, 0)])  6.14 us
    ppermute x5, waiting for transfers between devices, sibling(): return lax.ppermute(block, 'core', [(0, 1), (1, 0)])  2.79 us
  transfers between devices with their start and end apart: 15, of which 8 were waited for; matrix products, arithmetic and copies ran while one was open for 2% of the time, Pallas kernels for 27%

profile of v3, /device:TPU:1, one launch (start us, length us, event | category | flops | bytes accessed | tf_op | source)
XLA Modules:
  0.0 102.2 jit_solution(10593681255662765000)
XLA Ops:
  0.6 0.0 copy-start
  0.6 2.1 %collective-permute-start = (bf16[8,8192]{1,0:T(8,128)(2,1)}, bf16[8,8192]{1,0:T(8,128)(2,1)S(1)}, u32[]{:S(2)}, u32[]{:S(2)}) collective-permute-start(bf16[8,8192]{1,0:T(8,128)(2,1)} %param.7), channel_id=1, source_target_pairs={{0,1},{4,5},{8,9},{12,13},{1,2},{5,6},{9,10},{13,14},{2,3},{6,7},{... | collective-permute-start | bytes 393224 | tf_op jit(solution)/shard_map/ppermute | solution.py:35
  2.8 2.5 %collective-permute-start.1 = (bf16[8,8192]{1,0:T(8,128)(2,1)}, bf16[8,8192]{1,0:T(8,128)(2,1)S(1)}, u32[]{:S(2)}, u32[]{:S(2)}) collective-permute-start(bf16[8,8192]{1,0:T(8,128)(2,1)} %param.7), channel_id=1, source_target_pairs={{0,2},{4,6},{8,10},{12,14},{1,3},{5,7},{9,11},{13,15},{2,0},{6,4},... | collective-permute-start | bytes 393224 | tf_op jit(solution)/shard_map/ppermute | solution.py:35
  5.2 1.2 %collective-permute-start.2 = (bf16[8,8192]{1,0:T(8,128)(2,1)}, bf16[8,8192]{1,0:T(8,128)(2,1)S(1)}, u32[]{:S(2)}, u32[]{:S(2)}) collective-permute-start(bf16[8,8192]{1,0:T(8,128)(2,1)} %param.7), channel_id=1, source_target_pairs={{0,3},{4,7},{8,11},{12,15},{1,0},{5,4},{9,8},{13,12},{2,1},{6,5},{... | collective-permute-start | bytes 393224 | tf_op jit(solution)/shard_map/ppermute | solution.py:35
  6.4 0.7 convert_element_type.3.refs_3_
  7.1 0.0 copy-done
  7.1 0.7 add_bitcast_fusion.code_ref
  7.8 0.0 collective-permute-done
  7.8 1.7 %collective-permute-done.1 = bf16[8,8192]{1,0:T(8,128)(2,1)S(1)} collective-permute-done((bf16[8,8192]{1,0:T(8,128)(2,1)}, bf16[8,8192]{1,0:T(8,128)(2,1)S(1)}, u32[]{:S(2)}, u32[]{:S(2)}) %collective-permute-start.1) | collective-permute-done | bytes 131104 | tf_op jit(solution)/shard_map/ppermute | solution.py:35
  9.5 0.1 collective-permute-done.2
  9.5 0.9 pad_maximum_fusion.1
  10.5 1.7 %collective-permute-start.3 = (bf16[32,8192]{1,0:T(8,128)(2,1)S(1)}, bf16[32,8192]{1,0:T(8,128)(2,1)S(1)}, u32[]{:S(2)}, u32[]{:S(2)}) collective-permute-start(bf16[32,8192]{1,0:T(8,128)(2,1)S(1)} %pad_maximum_fusion.1), channel_id=1, source_target_pairs={{0,16},{4,20},{8,24},{12,28},{1,17},{5,21},{9,25},{13,29},{2,18},{... | collective-permute-start | bytes 1572872 | tf_op jit(solution)/shard_map/ppermute | solution.py:35
  12.2 3.3 %collective-permute-start.4 = (bf16[32,8192]{1,0:T(8,128)(2,1)S(1)}, bf16[32,8192]{1,0:T(8,128)(2,1)S(1)}, u32[]{:S(2)}, u32[]{:S(2)}) collective-permute-start(bf16[32,8192]{1,0:T(8,128)(2,1)S(1)} %pad_maximum_fusion.1), channel_id=1, source_target_pairs={{0,64},{4,68},{8,72},{12,76},{1,65},{5,69},{9,73},{13,77},{2,66},{... | collective-permute-start | bytes 1572872 | tf_op jit(solution)/shard_map/ppermute | solution.py:35
  15.5 0.7 collective-permute-start.5
  16.2 0.0 copy-start.1
  16.2 0.8 copy-done.1
  17.0 6.4 %shard_map.86 = (bf16[2,8192,512]{2,1,0:T(8,128)(2,1)S(1)}, s32[1024,128]{1,0:T(8,128)S(1)}) custom-call(bf16[8192,512]{1,0:T(8,128)(2,1)} %bitcast.11, bf16[8192,512]{1,0:T(8,128)(2,1)} %bitcast.12, f32[1,8192]{1,0:T(1,128)S(1)} %copy-done.1, s32[8,128]{1,0:T(8,128)S(1)} %add_bitcast_fusion.code_ref), custom_call_target="tpu_custom_call" | custom-call | flops 8388608 | bytes 16777216 | tf_op jit(solution)/shard_map/pallas_call | solution.py:70
  23.4 0.0 collective-permute-done.3
  23.4 4.6 %collective-permute-done.4 = bf16[32,8192]{1,0:T(8,128)(2,1)S(1)} collective-permute-done((bf16[32,8192]{1,0:T(8,128)(2,1)S(1)}, bf16[32,8192]{1,0:T(8,128)(2,1)S(1)}, u32[]{:S(2)}, u32[]{:S(2)}) %collective-permute-start.4) | collective-permute-done | bytes 524320 | tf_op jit(solution)/shard_map/ppermute | solution.py:35
  28.0 0.0 collective-permute-done.5
  28.0 0.2 pad_maximum_fusion.refs_0_
  28.1 2.0 %collective-permute-start.8 = (bf16[128,8192]{1,0:T(8,128)(2,1)S(1)}, bf16[128,8192]{1,0:T(8,128)(2,1)S(1)}, u32[]{:S(2)}, u32[]{:S(2)}) collective-permute-start(bf16[128,8192]{1,0:T(8,128)(2,1)S(1)} %pad_maximum_fusion.refs_0_), channel_id=1, source_target_pairs={{0,32},{32,0},{1,33},{33,1},{2,34},{34,2},{3,35},{35,3},{4,36},{36... | collective-permute-start | bytes 6291464 | tf_op jit(solution)/shard_map/ppermute | solution.py:39
  30.2 0.7 collective-permute-start.6
  30.9 1.9 %collective-permute-start.7 = (bf16[128,8192]{1,0:T(8,128)(2,1)S(1)}, bf16[128,8192]{1,0:T(8,128)(2,1)S(1)}, u32[]{:S(2)}, u32[]{:S(2)}) collective-permute-start(bf16[128,8192]{1,0:T(8,128)(2,1)S(1)} %pad_maximum_fusion.refs_0_), channel_id=1, source_target_pairs={{0,12},{4,0},{8,4},{12,8},{1,13},{5,1},{9,5},{13,9},{2,14},{6,2},{... | collective-permute-start | bytes 6291464 | tf_op jit(solution)/shard_map/ppermute | solution.py:35
  32.8 1.1 %collective-permute-done.8.refs_1_ = bf16[128,8192]{1,0:T(8,128)(2,1)S(1)} collective-permute-done((bf16[128,8192]{1,0:T(8,128)(2,1)S(1)}, bf16[128,8192]{1,0:T(8,128)(2,1)S(1)}, u32[]{:S(2)}, u32[]{:S(2)}) %collective-permute-start.8) | collective-permute-done | bytes 2097184 | tf_op jit(solution)/shard_map/ppermute | solution.py:39
  33.9 5.8 %shard_map.87.refs_6_ = f32[128,128]{1,0:T(8,128)S(1)} custom-call(bf16[128,8192]{1,0:T(8,128)(2,1)S(1)} %pad_maximum_fusion.refs_0_, bf16[128,8192]{1,0:T(8,128)(2,1)S(1)} %collective-permute-done.8.refs_1_, bf16[2,8192,512]{2,1,0:T(8,128)(2,1)S(1)} %get-tuple-element.27.refs_2_, f32[1,512]{1,0:T(1,128)S(1)} %convert_element_type.3.refs_3_, ...), custom_call_target="tpu_custom_call" | custom-call | flops 4294967296 | bytes 16777216 | tf_op jit(solution)/shard_map/pallas_call | solution.py:132
  39.8 16.8 %collective-permute-done.6.refs_0_ = bf16[128,8192]{1,0:T(8,128)(2,1)S(1)} collective-permute-done((bf16[128,8192]{1,0:T(8,128)(2,1)S(1)}, bf16[128,8192]{1,0:T(8,128)(2,1)S(1)}, u32[]{:S(2)}, u32[]{:S(2)}) %collective-permute-start.6) | collective-permute-done | bytes 2097184 | tf_op jit(solution)/shard_map/ppermute | solution.py:35
  56.5 0.0 collective-permute-done.7.refs_0_
  56.5 1.7 %collective-permute-start.12 = (bf16[128,8192]{1,0:T(8,128)(2,1)S(1)}, bf16[128,8192]{1,0:T(8,128)(2,1)S(1)}, u32[]{:S(2)}, u32[]{:S(2)}) collective-permute-start(bf16[128,8192]{1,0:T(8,128)(2,1)S(1)} %collective-permute-done.6.refs_0_), channel_id=1, source_target_pairs={{0,32},{32,0},{1,33},{33,1},{2,34},{34,2},{3,35},{35,3},{4,36},{36... | collective-permute-start | bytes 6291464 | tf_op jit(solution)/shard_map/ppermute | solution.py:39
  58.3 0.0 collective-permute-start.11
  58.3 0.1 slice.7
  58.4 0.1 slice.6
  58.4 2.3 %collective-permute-start.10 = (bf16[64,8192]{1,0:T(8,128)(2,1)S(1)}, bf16[64,8192]{1,0:T(8,128)(2,1)S(1)}, u32[]{:S(2)}, u32[]{:S(2)}) collective-permute-start(bf16[64,8192]{1,0:T(8,128)(2,1)S(1)} %slice.7), channel_id=1, source_target_pairs={{0,12},{4,0},{8,4},{12,8},{1,13},{5,1},{9,5},{13,9},{2,14},{6,2},{... | collective-permute-start | bytes 3145736 | tf_op jit(solution)/shard_map/ppermute | solution.py:35
  60.8 0.0 collective-permute-start.9
  60.8 1.3 %collective-permute-done.12.refs_1_ = bf16[128,8192]{1,0:T(8,128)(2,1)S(1)} collective-permute-done((bf16[128,8192]{1,0:T(8,128)(2,1)S(1)}, bf16[128,8192]{1,0:T(8,128)(2,1)S(1)}, u32[]{:S(2)}, u32[]{:S(2)}) %collective-permute-start.12) | collective-permute-done | bytes 2097184 | tf_op jit(solution)/shard_map/ppermute | solution.py:39
  62.1 5.8 %shard_map.88.refs_6_ = f32[128,128]{1,0:T(8,128)S(1)} custom-call(bf16[128,8192]{1,0:T(8,128)(2,1)S(1)} %collective-permute-done.6.refs_0_, bf16[128,8192]{1,0:T(8,128)(2,1)S(1)} %collective-permute-done.12.refs_1_, bf16[2,8192,512]{2,1,0:T(8,128)(2,1)S(1)} %get-tuple-element.27.refs_2_, f32[1,512]{1,0:T(1,128)S(1)} %convert_element_type.3.refs_3_, ...), custom_call_target="tpu_custom_call" | custom-call | flops 4294967296 | bytes 16777216 | tf_op jit(solution)/shard_map/pallas_call | solution.py:132
  67.9 0.0 collective-permute-done.11.refs_1_
  67.9 5.8 %shard_map.89.refs_6_ = f32[128,128]{1,0:T(8,128)S(1)} custom-call(bf16[128,8192]{1,0:T(8,128)(2,1)S(1)} %collective-permute-done.7.refs_0_, bf16[128,8192]{1,0:T(8,128)(2,1)S(1)} %collective-permute-done.11.refs_1_, bf16[2,8192,512]{2,1,0:T(8,128)(2,1)S(1)} %get-tuple-element.27.refs_2_, f32[1,512]{1,0:T(1,128)S(1)} %convert_element_type.3.refs_3_, ...), custom_call_target="tpu_custom_call" | custom-call | flops 4294967296 | bytes 16777216 | tf_op jit(solution)/shard_map/pallas_call | solution.py:132
  73.7 0.0 collective-permute-done.10.refs_1_
  73.7 2.2 %collective-permute-done.9.refs_0_ = bf16[64,8192]{1,0:T(8,128)(2,1)S(1)} collective-permute-done((bf16[64,8192]{1,0:T(8,128)(2,1)S(1)}, bf16[64,8192]{1,0:T(8,128)(2,1)S(1)}, u32[]{:S(2)}, u32[]{:S(2)}) %collective-permute-start.9) | collective-permute-done | bytes 1048608 | tf_op jit(solution)/shard_map/ppermute | solution.py:35
  75.9 2.4 %collective-permute-start.13 = (bf16[64,8192]{1,0:T(8,128)(2,1)S(1)}, bf16[64,8192]{1,0:T(8,128)(2,1)S(1)}, u32[]{:S(2)}, u32[]{:S(2)}) collective-permute-start(bf16[64,8192]{1,0:T(8,128)(2,1)S(1)} %collective-permute-done.9.refs_0_), channel_id=1, source_target_pairs={{0,32},{32,0},{1,33},{33,1},{2,34},{34,2},{3,35},{35,3},{4,36},{36... | collective-permute-start | bytes 3145736 | tf_op jit(solution)/shard_map/ppermute | solution.py:39
  78.3 0.0 collective-permute-start.14
  78.3 3.4 %shard_map.90.refs_6_ = f32[128,128]{1,0:T(8,128)S(1)} custom-call(bf16[64,8192]{1,0:T(8,128)(2,1)S(1)} %collective-permute-done.9.refs_0_, bf16[64,8192]{1,0:T(8,128)(2,1)S(1)} %collective-permute-done.10.refs_1_, bf16[2,8192,512]{2,1,0:T(8,128)(2,1)S(1)} %get-tuple-element.27.refs_2_, f32[1,512]{1,0:T(1,128)S(1)} %convert_element_type.3.refs_3_, ...), custom_call_target="tpu_custom_call" | custom-call | flops 2147483648 | bytes 16777216 | tf_op jit(solution)/shard_map/pallas_call | solution.py:132
  81.7 0.0 collective-permute-done.13.refs_0_
  81.7 0.4 collective-permute-done.14.refs_1_
  82.1 3.4 %shard_map.91 = f32[128,128]{1,0:T(8,128)S(1)} custom-call(bf16[64,8192]{1,0:T(8,128)(2,1)S(1)} %collective-permute-done.13.refs_0_, bf16[64,8192]{1,0:T(8,128)(2,1)S(1)} %collective-permute-done.14.refs_1_, bf16[2,8192,512]{2,1,0:T(8,128)(2,1)S(1)} %get-tuple-element.27.refs_2_, f32[1,512]{1,0:T(1,128)S(1)} %convert_element_type.3.refs_3_, ...), custom_call_target="tpu_custom_call" | custom-call | flops 2147483648 | bytes 16777216 | tf_op jit(solution)/shard_map/pallas_call | solution.py:132
  85.5 15.5 %all_to_all.5 = f32[128,1,128]{2,1,0:T(1,128)S(1)} all-to-all(f32[128,1,128]{2,1,0:T(1,128)S(1)} %bitcast.10), channel_id=1, replica_groups=mesh['xh'=2,'core'=2,'xl'=2,'z'=4,'y'=4] {'xh','core','xl','z','y'}, dimensions={0} | all-to-all | bytes 131072 | tf_op jit(solution)/shard_map/all_to_all | solution.py:185
  101.0 1.2 %shard_map.92 = (f32[1,32]{1,0:T(1,128)}, f32[4,8]{1,0:T(4,128)}) custom-call(f32[128,128]{1,0:T(8,128)S(1)} %bitcast.9, s32[256]{0:T(256)S(1)} %concatenate.10.refs_5_.unit_ref), custom_call_target="tpu_custom_call" | custom-call | tf_op jit(solution)/shard_map/pallas_call | solution.py:175
  (4 shorter events, 0.0 us)
Async XLA Ops:
  0.6 6.5 %copy-start = (s32[4,1024]{1,0:T(4,128)S(1)}, s32[4,1024]{1,0:T(4,128)}, u32[]{:S(2)}) copy-start(s32[4,1024]{1,0:T(4,128)} %param.12) | copy-start | bytes 49156
  0.6 7.2 %collective-permute-start = (bf16[8,8192]{1,0:T(8,128)(2,1)}, bf16[8,8192]{1,0:T(8,128)(2,1)S(1)}, u32[]{:S(2)}, u32[]{:S(2)}) collective-permute-start(bf16[8,8192]{1,0:T(8,128)(2,1)} %param.7), channel_id=1, source_target_pairs={{0,1},{4,5},{8,9},{12,13},{1,2},{5,6},{9,10},{13,14},{2,3},{6,7},{... | collective-permute-start | bytes 393224 | tf_op jit(solution)/shard_map/ppermute | solution.py:35
  2.8 6.7 %collective-permute-start.1 = (bf16[8,8192]{1,0:T(8,128)(2,1)}, bf16[8,8192]{1,0:T(8,128)(2,1)S(1)}, u32[]{:S(2)}, u32[]{:S(2)}) collective-permute-start(bf16[8,8192]{1,0:T(8,128)(2,1)} %param.7), channel_id=1, source_target_pairs={{0,2},{4,6},{8,10},{12,14},{1,3},{5,7},{9,11},{13,15},{2,0},{6,4},... | collective-permute-start | bytes 393224 | tf_op jit(solution)/shard_map/ppermute | solution.py:35
  5.2 4.3 %collective-permute-start.2 = (bf16[8,8192]{1,0:T(8,128)(2,1)}, bf16[8,8192]{1,0:T(8,128)(2,1)S(1)}, u32[]{:S(2)}, u32[]{:S(2)}) collective-permute-start(bf16[8,8192]{1,0:T(8,128)(2,1)} %param.7), channel_id=1, source_target_pairs={{0,3},{4,7},{8,11},{12,15},{1,0},{5,4},{9,8},{13,12},{2,1},{6,5},{... | collective-permute-start | bytes 393224 | tf_op jit(solution)/shard_map/ppermute | solution.py:35
  10.5 12.9 %collective-permute-start.3 = (bf16[32,8192]{1,0:T(8,128)(2,1)S(1)}, bf16[32,8192]{1,0:T(8,128)(2,1)S(1)}, u32[]{:S(2)}, u32[]{:S(2)}) collective-permute-start(bf16[32,8192]{1,0:T(8,128)(2,1)S(1)} %pad_maximum_fusion.1), channel_id=1, source_target_pairs={{0,16},{4,20},{8,24},{12,28},{1,17},{5,21},{9,25},{13,29},{2,18},{... | collective-permute-start | bytes 1572872 | tf_op jit(solution)/shard_map/ppermute | solution.py:35
  12.2 15.8 %collective-permute-start.4 = (bf16[32,8192]{1,0:T(8,128)(2,1)S(1)}, bf16[32,8192]{1,0:T(8,128)(2,1)S(1)}, u32[]{:S(2)}, u32[]{:S(2)}) collective-permute-start(bf16[32,8192]{1,0:T(8,128)(2,1)S(1)} %pad_maximum_fusion.1), channel_id=1, source_target_pairs={{0,64},{4,68},{8,72},{12,76},{1,65},{5,69},{9,73},{13,77},{2,66},{... | collective-permute-start | bytes 1572872 | tf_op jit(solution)/shard_map/ppermute | solution.py:35
  15.5 12.5 %collective-permute-start.5 = (bf16[32,8192]{1,0:T(8,128)(2,1)S(1)}, bf16[32,8192]{1,0:T(8,128)(2,1)S(1)}, u32[]{:S(2)}, u32[]{:S(2)}) collective-permute-start(bf16[32,8192]{1,0:T(8,128)(2,1)S(1)} %pad_maximum_fusion.1), channel_id=1, source_target_pairs={{0,80},{4,84},{8,88},{12,92},{1,81},{5,85},{9,89},{13,93},{2,82},{... | collective-permute-start | bytes 1572872 | tf_op jit(solution)/shard_map/ppermute | solution.py:35
  16.2 0.8 copy-start.1
  28.1 5.8 %collective-permute-start.8 = (bf16[128,8192]{1,0:T(8,128)(2,1)S(1)}, bf16[128,8192]{1,0:T(8,128)(2,1)S(1)}, u32[]{:S(2)}, u32[]{:S(2)}) collective-permute-start(bf16[128,8192]{1,0:T(8,128)(2,1)S(1)} %pad_maximum_fusion.refs_0_), channel_id=1, source_target_pairs={{0,32},{32,0},{1,33},{33,1},{2,34},{34,2},{3,35},{35,3},{4,36},{36... | collective-permute-start | bytes 6291464 | tf_op jit(solution)/shard_map/ppermute | solution.py:39
  30.2 26.4 %collective-permute-start.6 = (bf16[128,8192]{1,0:T(8,128)(2,1)S(1)}, bf16[128,8192]{1,0:T(8,128)(2,1)S(1)}, u32[]{:S(2)}, u32[]{:S(2)}) collective-permute-start(bf16[128,8192]{1,0:T(8,128)(2,1)S(1)} %pad_maximum_fusion.refs_0_), channel_id=1, source_target_pairs={{0,4},{4,8},{8,12},{12,0},{1,5},{5,9},{9,13},{13,1},{2,6},{6,10},{... | collective-permute-start | bytes 6291464 | tf_op jit(solution)/shard_map/ppermute | solution.py:35
  30.9 25.7 %collective-permute-start.7 = (bf16[128,8192]{1,0:T(8,128)(2,1)S(1)}, bf16[128,8192]{1,0:T(8,128)(2,1)S(1)}, u32[]{:S(2)}, u32[]{:S(2)}) collective-permute-start(bf16[128,8192]{1,0:T(8,128)(2,1)S(1)} %pad_maximum_fusion.refs_0_), channel_id=1, source_target_pairs={{0,12},{4,0},{8,4},{12,8},{1,13},{5,1},{9,5},{13,9},{2,14},{6,2},{... | collective-permute-start | bytes 6291464 | tf_op jit(solution)/shard_map/ppermute | solution.py:35
  56.5 5.5 %collective-permute-start.12 = (bf16[128,8192]{1,0:T(8,128)(2,1)S(1)}, bf16[128,8192]{1,0:T(8,128)(2,1)S(1)}, u32[]{:S(2)}, u32[]{:S(2)}) collective-permute-start(bf16[128,8192]{1,0:T(8,128)(2,1)S(1)} %collective-permute-done.6.refs_0_), channel_id=1, source_target_pairs={{0,32},{32,0},{1,33},{33,1},{2,34},{34,2},{3,35},{35,3},{4,36},{36... | collective-permute-start | bytes 6291464 | tf_op jit(solution)/shard_map/ppermute | solution.py:39
  58.3 9.6 %collective-permute-start.11 = (bf16[128,8192]{1,0:T(8,128)(2,1)S(1)}, bf16[128,8192]{1,0:T(8,128)(2,1)S(1)}, u32[]{:S(2)}, u32[]{:S(2)}) collective-permute-start(bf16[128,8192]{1,0:T(8,128)(2,1)S(1)} %collective-permute-done.7.refs_0_), channel_id=1, source_target_pairs={{0,32},{32,0},{1,33},{33,1},{2,34},{34,2},{3,35},{35,3},{4,36},{36... | collective-permute-start | bytes 6291464 | tf_op jit(solution)/shard_map/ppermute | solution.py:39
  58.4 15.3 %collective-permute-start.10 = (bf16[64,8192]{1,0:T(8,128)(2,1)S(1)}, bf16[64,8192]{1,0:T(8,128)(2,1)S(1)}, u32[]{:S(2)}, u32[]{:S(2)}) collective-permute-start(bf16[64,8192]{1,0:T(8,128)(2,1)S(1)} %slice.7), channel_id=1, source_target_pairs={{0,12},{4,0},{8,4},{12,8},{1,13},{5,1},{9,5},{13,9},{2,14},{6,2},{... | collective-permute-start | bytes 3145736 | tf_op jit(solution)/shard_map/ppermute | solution.py:35
  60.8 15.2 %collective-permute-start.9 = (bf16[64,8192]{1,0:T(8,128)(2,1)S(1)}, bf16[64,8192]{1,0:T(8,128)(2,1)S(1)}, u32[]{:S(2)}, u32[]{:S(2)}) collective-permute-start(bf16[64,8192]{1,0:T(8,128)(2,1)S(1)} %slice.6), channel_id=1, source_target_pairs={{0,4},{4,8},{8,12},{12,0},{1,5},{5,9},{9,13},{13,1},{2,6},{6,10},{... | collective-permute-start | bytes 3145736 | tf_op jit(solution)/shard_map/ppermute | solution.py:35
  75.9 5.8 %collective-permute-start.13 = (bf16[64,8192]{1,0:T(8,128)(2,1)S(1)}, bf16[64,8192]{1,0:T(8,128)(2,1)S(1)}, u32[]{:S(2)}, u32[]{:S(2)}) collective-permute-start(bf16[64,8192]{1,0:T(8,128)(2,1)S(1)} %collective-permute-done.9.refs_0_), channel_id=1, source_target_pairs={{0,32},{32,0},{1,33},{33,1},{2,34},{34,2},{3,35},{35,3},{4,36},{36... | collective-permute-start | bytes 3145736 | tf_op jit(solution)/shard_map/ppermute | solution.py:39
  78.3 3.8 %collective-permute-start.14 = (bf16[64,8192]{1,0:T(8,128)(2,1)S(1)}, bf16[64,8192]{1,0:T(8,128)(2,1)S(1)}, u32[]{:S(2)}, u32[]{:S(2)}) collective-permute-start(bf16[64,8192]{1,0:T(8,128)(2,1)S(1)} %collective-permute-done.10.refs_1_), channel_id=1, source_target_pairs={{0,32},{32,0},{1,33},{33,1},{2,34},{34,2},{3,35},{35,3},{4,36},{36... | collective-permute-start | bytes 3145736 | tf_op jit(solution)/shard_map/ppermute | solution.py:39

commit v4 on v3

--- a/solution.py
+++ b/solution.py
@@ -9,7 +9,7 @@
 
 epsilon = 1e-06
 ALL = ("xh", "core", "xl", "z", "y")
-ORDER = (("y", "x", "z"), ("x", "z", "y"))
+ORDER = (("y", "x", "z"), ("z", "x", "y"))
 FOLD = 1024
 SCOPED = 12 * 1024 * 1024
 
@@ -85,11 +85,11 @@
     first, squares = 0, []
     for ref in rows:
         count = ref.shape[0]
-        for at in range(0, count, 64):
-            total = jnp.zeros((64, 128), jnp.float32)
+        for at in range(0, count, 16):
+            total = jnp.zeros((16, 128), jnp.float32)
             for lane in range(0, features, 128):
-                part = ref[at : at + 64, lane : lane + 128]
-                block_ref[first + at : first + at + 64, lane : lane + 128] = part
+                part = ref[at : at + 16, lane : lane + 128]
+                block_ref[first + at : first + at + 16, lane : lane + 128] = part
                 part = part.astype(jnp.float32)
                 total = total + part * part
             squares.append(jnp.sum(total, axis=1, keepdims=True))
@@ -144,6 +144,12 @@
     return tuple(third * 32 + half * 16 + line * 4 + at for line in lines for at in range(4))
 
 
+def both(pieces, units, rest, sent):
+    others = [sibling(piece) for piece in pieces]
+    sent = stage(list(zip(pieces, units(0))), *rest, sent)
+    return stage(list(zip(others, units(1))), *rest, sent)
+
+
 def unit_table(core, section):
     place = {"x": lax.axis_index("xh") * 2 + lax.axis_index("xl"), "y": lax.axis_index("y"), "z": lax.axis_index("z")}
     at = jnp.arange(128, dtype=jnp.int32)
@@ -198,24 +204,52 @@
     line, gate, up, code, unit, head, sent = lax.optimization_barrier(
         (line, gate_weight[0], up_weight[0], code, unit, head, sent)
     )
-    plane = jnp.concatenate([line] + [shift(line, 1, step) for step in (1, 2, 3)], axis=0)
+    left, right = shift(line, 1, 1), shift(line, 1, 3)
+    down, above = shift(line, 2, 1), shift(line, 2, 3)
     weight, code = fold(gate, up, norm_gain, code)
-    plane, weight, code = lax.optimization_barrier((plane, weight, code))
+    to_up = jnp.concatenate([left, right, down[:16]], axis=0)
+    to_down = jnp.concatenate([left, right, above[16:]], axis=0)
+    remainder = jnp.concatenate([down[16:], above], axis=0)
+    other_line = sibling(line)
+    line, other_line, remainder, to_up, to_down, weight, code = lax.optimization_barrier(
+        (line, other_line, remainder, to_up, to_down, weight, code)
+    )
     rest = (weight, head, code, unit)
-    every = (0, 1, 2, 3)
-    other = sibling(plane)
-    behind = shift(plane, 2, 1)
-    ahead = shift(plane, 2, 3)
-    sent = stage(((plane, held(0, 0, every)), (other, held(1, 0, every))), *rest, sent)
-    behind, ahead, sent = lax.optimization_barrier((behind, ahead, sent))
-    far_low = shift(behind[:64], 2, 1)
-    far_high = shift(ahead[64:], 2, 3)
-    sent = stage(((behind, held(0, 1, every)), (sibling(behind), held(1, 1, every))), *rest, sent)
-    sent = stage(((ahead, held(0, 3, every)), (sibling(ahead), held(1, 3, every))), *rest, sent)
-    far_low, far_high, sent = lax.optimization_barrier((far_low, far_high, sent))
-    far = ((sibling(far_low), held(1, 2, (0, 1))), (sibling(far_high), held(1, 2, (2, 3))))
-    sent = stage(((far_low, held(0, 2, (0, 1))), (far_high, held(0, 2, (2, 3)))), *rest, sent)
-    sent = stage(far, *rest, sent)
+
+    across = shift(line, 1, 2)
+    from_down, from_up = shift(to_up, 2, 1), shift(to_down, 2, 3)
+    near = held(0, 0, (0,)), held(0, 0, (1, 3)) + held(0, 1, (0,))[:2], held(0, 1, (0,))[2:] + held(0, 3, (0,))
+    other_near = held(1, 0, (0,)), held(1, 0, (1, 3)) + held(1, 1, (0,))[:2], held(1, 1, (0,))[2:] + held(1, 3, (0,))
+    others = (other_line, sibling(to_up), sibling(remainder))
+    sent = stage(list(zip((line, to_up, remainder), near)), *rest, sent)
+    sent = stage(list(zip(others, other_near)), *rest, sent)
+    across, from_down, from_up, sent = lax.optimization_barrier((across, from_down, from_up, sent))
+
+    far = shift(jnp.concatenate([from_down[64:], from_up[64:]], axis=0), 1, 2)
+    low = shift(jnp.concatenate([across, from_down[:32]], axis=0), 2, 1)
+    high = shift(jnp.concatenate([across, from_up[32:64]], axis=0), 2, 3)
+    own = (from_down, from_up, across)
+    sent = both(
+        own,
+        lambda half: [
+            held(half, 1, (1, 3)) + held(half, 2, (0,))[:2],
+            held(half, 3, (1, 3)) + held(half, 2, (0,))[2:],
+            held(half, 0, (2,)),
+        ],
+        rest,
+        sent,
+    )
+    low, high, far, sent = lax.optimization_barrier((low, high, far, sent))
+    sent = both(
+        (low, high, far),
+        lambda half: [
+            held(half, 1, (2,)) + held(half, 2, (1,)),
+            held(half, 3, (2,)) + held(half, 2, (3,)),
+            held(half, 2, (2,)),
+        ],
+        rest,
+        sent,
+    )
 
     return finish(exchange(sent), unit)
 

time: 102 us -> 97.4 us (0.955)
  waiting for transfers between devices: 28.1 us -> 13.1 us
  starting transfers between devices: 22.6 us -> 31.6 us
  Pallas kernels: 31.7 us -> 32.9 us
    ppermute x10 -> x13, waiting for transfers between devices: 25.3 us -> 11.7 us  [shift(): return lax.ppermute(block, ALL, shift_pairs(phase, step))]
    ppermute x10 -> x13, starting transfers between devices: 16.5 us -> 21.2 us  [shift(): return lax.ppermute(block, ALL, shift_pairs(phase, step))]
    ppermute x5 -> x9, starting transfers between devices: 6.14 us -> 10.4 us  [sibling(): return lax.ppermute(block, 'core', [(0, 1), (1, 0)])]
    ppermute x5 -> x9, waiting for transfers between devices: 2.79 us -> 1.4 us  [sibling(): return lax.ppermute(block, 'core', [(0, 1), (1, 0)])]
    pallas_call x5 -> x6, Pallas kernels: 24.2 us -> 25.3 us  [stage(): pl.pallas_call(functools.partial(stage_kernel, units, len(arrays)), out_s...]
  transfers between devices with their start and end apart: 15 -> 22, of which waited for: 8 -> 7; matrix products, arithmetic and copies ran while one was open for 2% -> 2% of each run, Pallas kernels for 27% -> 29%
where the time goes in v4:
time: 97.4 us; the launch traced here: 97.1 us
  Pallas kernels  32.9 us (34%)
  starting transfers between devices  31.6 us (32%)
  blocking collectives  14.9 us (15%)
  waiting for transfers between devices  13.1 us (13%)
  other arithmetic  2.81 us (3%)
    pallas_call x6, Pallas kernels, stage(): pl.pallas_call(functools.partial(stage_kernel, units, len(arrays)), out_s...  25.3 us
    ppermute x13, starting transfers between devices, shift(): return lax.ppermute(block, ALL, shift_pairs(phase, step))  21.2 us
    all_to_all x1, blocking collectives, exchange(): lax.all_to_all(sent[:, None, :], ALL, split_axis=0, concat_axis=0, tiled=...  14.9 us
    ppermute x13, waiting for transfers between devices, shift(): return lax.ppermute(block, ALL, shift_pairs(phase, step))  11.7 us
    ppermute x9, starting transfers between devices, sibling(): return lax.ppermute(block, 'core', [(0, 1), (1, 0)])  10.4 us
    pallas_call x1, Pallas kernels, fold(): pl.pallas_call(fold_kernel, out_shape=(pltpu.VMEM((2, features, width), j...  6.38 us
  transfers between devices with their start and end apart: 22, of which 7 were waited for; matrix products, arithmetic and copies ran while one was open for 2% of the time, Pallas kernels for 29%

profile of v4, /device:TPU:1, one launch (start us, length us, event | category | flops | bytes accessed | tf_op | source)
XLA Modules:
  0.0 97.1 jit_solution(14601026143846711793)
XLA Ops:
  0.6 0.0 copy-start
  0.6 2.5 %collective-permute-start = (bf16[8,8192]{1,0:T(8,128)(2,1)}, bf16[8,8192]{1,0:T(8,128)(2,1)S(1)}, u32[]{:S(2)}, u32[]{:S(2)}) collective-permute-start(bf16[8,8192]{1,0:T(8,128)(2,1)} %param.7), channel_id=1, source_target_pairs={{0,1},{4,5},{8,9},{12,13},{1,2},{5,6},{9,10},{13,14},{2,3},{6,7},{... | collective-permute-start | bytes 393224 | tf_op jit(solution)/shard_map/ppermute | solution.py:35
  3.2 3.3 %collective-permute-start.1 = (bf16[8,8192]{1,0:T(8,128)(2,1)}, bf16[8,8192]{1,0:T(8,128)(2,1)S(1)}, u32[]{:S(2)}, u32[]{:S(2)}) collective-permute-start(bf16[8,8192]{1,0:T(8,128)(2,1)} %param.7), channel_id=1, source_target_pairs={{0,2},{4,6},{8,10},{12,14},{1,3},{5,7},{9,11},{13,15},{2,0},{6,4},... | collective-permute-start | bytes 393224 | tf_op jit(solution)/shard_map/ppermute | solution.py:35
  6.5 0.7 collective-permute-start.2
  7.2 0.7 convert_element_type.3.refs_4_
  8.0 0.7 add_bitcast_fusion.code_ref
  8.6 0.0 collective-permute-done
  8.6 2.1 %collective-permute-done.1 = bf16[8,8192]{1,0:T(8,128)(2,1)S(1)} collective-permute-done((bf16[8,8192]{1,0:T(8,128)(2,1)}, bf16[8,8192]{1,0:T(8,128)(2,1)S(1)}, u32[]{:S(2)}, u32[]{:S(2)}) %collective-permute-start.1) | collective-permute-done | bytes 131104 | tf_op jit(solution)/shard_map/ppermute | solution.py:35
  10.7 0.1 collective-permute-done.2
  10.8 0.9 pad_maximum_fusion.6.refs_0_
  11.7 1.4 %collective-permute-start.4 = (bf16[32,8192]{1,0:T(8,128)(2,1)S(1)}, bf16[32,8192]{1,0:T(8,128)(2,1)S(1)}, u32[]{:S(2)}, u32[]{:S(2)}) collective-permute-start(bf16[32,8192]{1,0:T(8,128)(2,1)S(1)} %pad_maximum_fusion.6.refs_0_), channel_id=1, source_target_pairs={{0,4},{4,8},{8,12},{12,0},{1,5},{5,9},{9,13},{13,1},{2,6},{6,10},{... | collective-permute-start | bytes 1572872 | tf_op jit(solution)/shard_map/ppermute | solution.py:35
  13.1 1.5 %collective-permute-start.5 = (bf16[32,8192]{1,0:T(8,128)(2,1)S(1)}, bf16[32,8192]{1,0:T(8,128)(2,1)S(1)}, u32[]{:S(2)}, u32[]{:S(2)}) collective-permute-start(bf16[32,8192]{1,0:T(8,128)(2,1)S(1)} %pad_maximum_fusion.6.refs_0_), channel_id=1, source_target_pairs={{0,12},{4,0},{8,4},{12,8},{1,13},{5,1},{9,5},{13,9},{2,14},{6,2},{... | collective-permute-start | bytes 1572872 | tf_op jit(solution)/shard_map/ppermute | solution.py:35
  14.6 1.2 %collective-permute-start.6 = (bf16[32,8192]{1,0:T(8,128)(2,1)S(1)}, bf16[32,8192]{1,0:T(8,128)(2,1)S(1)}, u32[]{:S(2)}, u32[]{:S(2)}) collective-permute-start(bf16[32,8192]{1,0:T(8,128)(2,1)S(1)} %pad_maximum_fusion.6.refs_0_), channel_id=1, source_target_pairs={{0,16},{4,20},{8,24},{12,28},{1,17},{5,21},{9,25},{13,29},{2,18},{... | collective-permute-start | bytes 1572872 | tf_op jit(solution)/shard_map/ppermute | solution.py:35
  15.8 1.5 %collective-permute-start.7 = (bf16[32,8192]{1,0:T(8,128)(2,1)S(1)}, bf16[32,8192]{1,0:T(8,128)(2,1)S(1)}, u32[]{:S(2)}, u32[]{:S(2)}) collective-permute-start(bf16[32,8192]{1,0:T(8,128)(2,1)S(1)} %pad_maximum_fusion.6.refs_0_), channel_id=1, source_target_pairs={{0,80},{4,84},{8,88},{12,92},{1,81},{5,85},{9,89},{13,93},{2,82},{... | collective-permute-start | bytes 1572872 | tf_op jit(solution)/shard_map/ppermute | solution.py:35
  17.3 2.9 %collective-permute-start.3 = (bf16[32,8192]{1,0:T(8,128)(2,1)S(1)}, bf16[32,8192]{1,0:T(8,128)(2,1)S(1)}, u32[]{:S(2)}, u32[]{:S(2)}) collective-permute-start(bf16[32,8192]{1,0:T(8,128)(2,1)S(1)} %pad_maximum_fusion.6.refs_0_), channel_id=1, source_target_pairs={{0,32},{32,0},{1,33},{33,1},{2,34},{34,2},{3,35},{35,3},{4,36},{36... | collective-permute-start | bytes 1572872 | tf_op jit(solution)/shard_map/ppermute | solution.py:39
  20.2 0.8 copy-done.1
  21.0 6.4 %shard_map.86 = (bf16[2,8192,512]{2,1,0:T(8,128)(2,1)S(1)}, s32[1024,128]{1,0:T(8,128)S(1)}) custom-call(bf16[8192,512]{1,0:T(8,128)(2,1)} %bitcast.11, bf16[8192,512]{1,0:T(8,128)(2,1)} %bitcast.12, f32[1,8192]{1,0:T(1,128)S(1)} %copy-done.1, s32[8,128]{1,0:T(8,128)S(1)} %add_bitcast_fusion.code_ref), custom_call_target="tpu_custom_call" | custom-call | flops 8388608 | bytes 16777216 | tf_op jit(solution)/shard_map/pallas_call | solution.py:70
  27.5 0.0 collective-permute-done.6
  27.5 0.2 pad_maximum_fusion.2
  27.7 0.1 pad_maximum_fusion.5.refs_2_
  27.8 2.8 %collective-permute-start.11 = (bf16[80,8192]{1,0:T(8,128)(2,1)S(1)}, bf16[80,8192]{1,0:T(8,128)(2,1)S(1)}, u32[]{:S(2)}, u32[]{:S(2)}) collective-permute-start(bf16[80,8192]{1,0:T(8,128)(2,1)S(1)} %get-tuple-element.33.refs_1_), channel_id=1, source_target_pairs={{0,32},{32,0},{1,33},{33,1},{2,34},{34,2},{3,35},{35,3},{4,36},{36... | collective-permute-start | bytes 3932168 | tf_op jit(solution)/shard_map/ppermute | solution.py:39
  30.5 1.4 %collective-permute-start.10 = (bf16[80,8192]{1,0:T(8,128)(2,1)S(1)}, bf16[80,8192]{1,0:T(8,128)(2,1)S(1)}, u32[]{:S(2)}, u32[]{:S(2)}) collective-permute-start(bf16[80,8192]{1,0:T(8,128)(2,1)S(1)} %get-tuple-element.34), channel_id=1, source_target_pairs={{0,12},{4,0},{8,4},{12,8},{1,13},{5,1},{9,5},{13,9},{2,14},{6,2},{... | collective-permute-start | bytes 3932168 | tf_op jit(solution)/shard_map/ppermute | solution.py:35
  31.9 0.1 collective-permute-start.9
  32.0 0.6 collective-permute-start.12
  32.6 2.4 %collective-permute-start.8 = (bf16[32,8192]{1,0:T(8,128)(2,1)S(1)}, bf16[32,8192]{1,0:T(8,128)(2,1)S(1)}, u32[]{:S(2)}, u32[]{:S(2)}) collective-permute-start(bf16[32,8192]{1,0:T(8,128)(2,1)S(1)} %pad_maximum_fusion.6.refs_0_), channel_id=1, source_target_pairs={{0,64},{4,68},{8,72},{12,76},{1,65},{5,69},{9,73},{13,77},{2,66},{... | collective-permute-start | bytes 1572872 | tf_op jit(solution)/shard_map/ppermute | solution.py:35
  35.1 4.0 %shard_map.87.refs_7_ = f32[128,128]{1,0:T(8,128)S(1)} custom-call(bf16[32,8192]{1,0:T(8,128)(2,1)S(1)} %pad_maximum_fusion.6.refs_0_, bf16[80,8192]{1,0:T(8,128)(2,1)S(1)} %get-tuple-element.33.refs_1_, bf16[48,8192]{1,0:T(8,128)(2,1)S(1)} %pad_maximum_fusion.5.refs_2_, bf16[2,8192,512]{2,1,0:T(8,128)(2,1)S(1)} %get-tuple-element.37.refs_3_, ...), custom_call_target="tpu_custom_call" | custom-call | flops 2684354560 | bytes 16777216 | tf_op jit(solution)/shard_map/pallas_call | solution.py:132
  39.1 4.0 %shard_map.88.refs_7_ = f32[128,128]{1,0:T(8,128)S(1)} custom-call(bf16[32,8192]{1,0:T(8,128)(2,1)S(1)} %collective-permute-done.3.refs_0_, bf16[80,8192]{1,0:T(8,128)(2,1)S(1)} %collective-permute-done.11.refs_1_, bf16[48,8192]{1,0:T(8,128)(2,1)S(1)} %collective-permute-done.12.refs_2_, bf16[2,8192,512]{2,1,0:T(8,128)(2,1)S(1)} %get-tuple-element.37.refs_3_, ...), custom_call_target="tpu_custom_call" | custom-call | flops 2684354560 | bytes 16777216 | tf_op jit(solution)/shard_map/pallas_call | solution.py:132
  43.1 4.6 %collective-permute-done.8.refs_2_ = bf16[32,8192]{1,0:T(8,128)(2,1)S(1)} collective-permute-done((bf16[32,8192]{1,0:T(8,128)(2,1)S(1)}, bf16[32,8192]{1,0:T(8,128)(2,1)S(1)}, u32[]{:S(2)}, u32[]{:S(2)}) %collective-permute-start.8) | collective-permute-done | bytes 524320 | tf_op jit(solution)/shard_map/ppermute | solution.py:35
  47.7 2.2 %collective-permute-done.9.refs_0_ = bf16[80,8192]{1,0:T(8,128)(2,1)S(1)} collective-permute-done((bf16[80,8192]{1,0:T(8,128)(2,1)S(1)}, bf16[80,8192]{1,0:T(8,128)(2,1)S(1)}, u32[]{:S(2)}, u32[]{:S(2)}) %collective-permute-start.9) | collective-permute-done | bytes 1310752 | tf_op jit(solution)/shard_map/ppermute | solution.py:35
  49.9 1.5 %collective-permute-start.16 = (bf16[80,8192]{1,0:T(8,128)(2,1)S(1)}, bf16[80,8192]{1,0:T(8,128)(2,1)S(1)}, u32[]{:S(2)}, u32[]{:S(2)}) collective-permute-start(bf16[80,8192]{1,0:T(8,128)(2,1)S(1)} %collective-permute-done.9.refs_0_), channel_id=1, source_target_pairs={{0,32},{32,0},{1,33},{33,1},{2,34},{34,2},{3,35},{35,3},{4,36},{36... | collective-permute-start | bytes 3932168 | tf_op jit(solution)/shard_map/ppermute | solution.py:39
  51.4 0.3 collective-permute-start.17
  51.7 0.6 collective-permute-start.18
  52.3 0.2 pad_maximum_fusion.3
  52.6 0.1 collective-permute-start.13
  52.7 2.6 %collective-permute-start.14 = (bf16[64,8192]{1,0:T(8,128)(2,1)S(1)}, bf16[64,8192]{1,0:T(8,128)(2,1)S(1)}, u32[]{:S(2)}, u32[]{:S(2)}) collective-permute-start(bf16[64,8192]{1,0:T(8,128)(2,1)S(1)} %get-tuple-element.52), channel_id=1, source_target_pairs={{0,12},{4,0},{8,4},{12,8},{1,13},{5,1},{9,5},{13,9},{2,14},{6,2},{... | collective-permute-start | bytes 3145736 | tf_op jit(solution)/shard_map/ppermute | solution.py:35
  55.4 1.3 %collective-permute-done.18.refs_2_ = bf16[32,8192]{1,0:T(8,128)(2,1)S(1)} collective-permute-done((bf16[32,8192]{1,0:T(8,128)(2,1)S(1)}, bf16[32,8192]{1,0:T(8,128)(2,1)S(1)}, u32[]{:S(2)}, u32[]{:S(2)}) %collective-permute-start.18) | collective-permute-done | bytes 524320 | tf_op jit(solution)/shard_map/ppermute | solution.py:39
  56.7 2.4 %collective-permute-start.15 = (bf16[32,8192]{1,0:T(8,128)(2,1)S(1)}, bf16[32,8192]{1,0:T(8,128)(2,1)S(1)}, u32[]{:S(2)}, u32[]{:S(2)}) collective-permute-start(bf16[32,8192]{1,0:T(8,128)(2,1)S(1)} %pad_maximum_fusion.7), channel_id=1, source_target_pairs={{0,64},{4,68},{8,72},{12,76},{1,65},{5,69},{9,73},{13,77},{2,66},{... | collective-permute-start | bytes 1572872 | tf_op jit(solution)/shard_map/ppermute | solution.py:35
  59.1 4.7 %shard_map.89.refs_7_ = f32[128,128]{1,0:T(8,128)S(1)} custom-call(bf16[80,8192]{1,0:T(8,128)(2,1)S(1)} %collective-permute-done.9.refs_0_, bf16[80,8192]{1,0:T(8,128)(2,1)S(1)} %collective-permute-done.10.refs_1_, bf16[32,8192]{1,0:T(8,128)(2,1)S(1)} %collective-permute-done.8.refs_2_, bf16[2,8192,512]{2,1,0:T(8,128)(2,1)S(1)} %get-tuple-element.37.refs_3_, ...), custom_call_target="tpu_custom_call" | custom-call | flops 3221225472 | bytes 16777216 | tf_op jit(solution)/shard_map/pallas_call | solution.py:132
  63.8 4.7 %shard_map.90.refs_7_ = f32[128,128]{1,0:T(8,128)S(1)} custom-call(bf16[80,8192]{1,0:T(8,128)(2,1)S(1)} %collective-permute-done.16.refs_0_, bf16[80,8192]{1,0:T(8,128)(2,1)S(1)} %collective-permute-done.17.refs_1_, bf16[32,8192]{1,0:T(8,128)(2,1)S(1)} %collective-permute-done.18.refs_2_, bf16[2,8192,512]{2,1,0:T(8,128)(2,1)S(1)} %get-tuple-element.37.refs_3_, ...), custom_call_target="tpu_custom_call" | custom-call | flops 3221225472 | bytes 16777216 | tf_op jit(solution)/shard_map/pallas_call | solution.py:132
  68.5 2.8 %collective-permute-done.15.refs_2_ = bf16[32,8192]{1,0:T(8,128)(2,1)S(1)} collective-permute-done((bf16[32,8192]{1,0:T(8,128)(2,1)S(1)}, bf16[32,8192]{1,0:T(8,128)(2,1)S(1)}, u32[]{:S(2)}, u32[]{:S(2)}) %collective-permute-start.15) | collective-permute-done | bytes 524320 | tf_op jit(solution)/shard_map/ppermute | solution.py:35
  71.3 1.2 %collective-permute-start.19 = (bf16[64,8192]{1,0:T(8,128)(2,1)S(1)}, bf16[64,8192]{1,0:T(8,128)(2,1)S(1)}, u32[]{:S(2)}, u32[]{:S(2)}) collective-permute-start(bf16[64,8192]{1,0:T(8,128)(2,1)S(1)} %collective-permute-done.13.refs_0_), channel_id=1, source_target_pairs={{0,32},{32,0},{1,33},{33,1},{2,34},{34,2},{3,35},{35,3},{4,36},{36... | collective-permute-start | bytes 3145736 | tf_op jit(solution)/shard_map/ppermute | solution.py:39
  72.5 0.1 collective-permute-start.20
  72.6 0.4 collective-permute-start.21
  73.0 4.0 %shard_map.91.refs_7_ = f32[128,128]{1,0:T(8,128)S(1)} custom-call(bf16[64,8192]{1,0:T(8,128)(2,1)S(1)} %collective-permute-done.13.refs_0_, bf16[64,8192]{1,0:T(8,128)(2,1)S(1)} %collective-permute-done.14.refs_1_, bf16[32,8192]{1,0:T(8,128)(2,1)S(1)} %collective-permute-done.15.refs_2_, bf16[2,8192,512]{2,1,0:T(8,128)(2,1)S(1)} %get-tuple-element.37.refs_3_, ...), custom_call_target="tpu_custom_call" | custom-call | flops 2684354560 | bytes 16777216 | tf_op jit(solution)/shard_map/pallas_call | solution.py:132
  77.0 0.1 collective-permute-done.21.refs_2_
  77.1 4.0 %shard_map.92 = f32[128,128]{1,0:T(8,128)S(1)} custom-call(bf16[64,8192]{1,0:T(8,128)(2,1)S(1)} %collective-permute-done.19.refs_0_, bf16[64,8192]{1,0:T(8,128)(2,1)S(1)} %collective-permute-done.20.refs_1_, bf16[32,8192]{1,0:T(8,128)(2,1)S(1)} %collective-permute-done.21.refs_2_, bf16[2,8192,512]{2,1,0:T(8,128)(2,1)S(1)} %get-tuple-element.37.refs_3_, ...), custom_call_target="tpu_custom_call" | custom-call | flops 2684354560 | bytes 16777216 | tf_op jit(solution)/shard_map/pallas_call | solution.py:132
  81.1 14.9 %all_to_all.5 = f32[128,1,128]{2,1,0:T(1,128)S(1)} all-to-all(f32[128,1,128]{2,1,0:T(1,128)S(1)} %bitcast.9), channel_id=1, replica_groups=mesh['xh'=2,'core'=2,'xl'=2,'z'=4,'y'=4] {'xh','core','xl','z','y'}, dimensions={0} | all-to-all | bytes 131072 | tf_op jit(solution)/shard_map/all_to_all | solution.py:191
  96.0 1.2 %shard_map.93 = (f32[1,32]{1,0:T(1,128)}, f32[4,8]{1,0:T(4,128)}) custom-call(f32[128,128]{1,0:T(8,128)S(1)} %bitcast.10, s32[256]{0:T(256)S(1)} %concatenate.25.refs_6_.unit_ref), custom_call_target="tpu_custom_call" | custom-call | tf_op jit(solution)/shard_map/pallas_call | solution.py:181
  (26 shorter events, 0.3 us)
Async XLA Ops:
  0.6 7.3 %copy-start = (s32[4,1024]{1,0:T(4,128)S(1)}, s32[4,1024]{1,0:T(4,128)}, u32[]{:S(2)}) copy-start(s32[4,1024]{1,0:T(4,128)} %param.12) | copy-start | bytes 49156
  0.6 8.0 %collective-permute-start = (bf16[8,8192]{1,0:T(8,128)(2,1)}, bf16[8,8192]{1,0:T(8,128)(2,1)S(1)}, u32[]{:S(2)}, u32[]{:S(2)}) collective-permute-start(bf16[8,8192]{1,0:T(8,128)(2,1)} %param.7), channel_id=1, source_target_pairs={{0,1},{4,5},{8,9},{12,13},{1,2},{5,6},{9,10},{13,14},{2,3},{6,7},{... | collective-permute-start | bytes 393224 | tf_op jit(solution)/shard_map/ppermute | solution.py:35
  3.2 7.6 %collective-permute-start.1 = (bf16[8,8192]{1,0:T(8,128)(2,1)}, bf16[8,8192]{1,0:T(8,128)(2,1)S(1)}, u32[]{:S(2)}, u32[]{:S(2)}) collective-permute-start(bf16[8,8192]{1,0:T(8,128)(2,1)} %param.7), channel_id=1, source_target_pairs={{0,2},{4,6},{8,10},{12,14},{1,3},{5,7},{9,11},{13,15},{2,0},{6,4},... | collective-permute-start | bytes 393224 | tf_op jit(solution)/shard_map/ppermute | solution.py:35
  6.5 4.3 %collective-permute-start.2 = (bf16[8,8192]{1,0:T(8,128)(2,1)}, bf16[8,8192]{1,0:T(8,128)(2,1)S(1)}, u32[]{:S(2)}, u32[]{:S(2)}) collective-permute-start(bf16[8,8192]{1,0:T(8,128)(2,1)} %param.7), channel_id=1, source_target_pairs={{0,3},{4,7},{8,11},{12,15},{1,0},{5,4},{9,8},{13,12},{2,1},{6,5},{... | collective-permute-start | bytes 393224 | tf_op jit(solution)/shard_map/ppermute | solution.py:35
  11.7 15.6 %collective-permute-start.4 = (bf16[32,8192]{1,0:T(8,128)(2,1)S(1)}, bf16[32,8192]{1,0:T(8,128)(2,1)S(1)}, u32[]{:S(2)}, u32[]{:S(2)}) collective-permute-start(bf16[32,8192]{1,0:T(8,128)(2,1)S(1)} %pad_maximum_fusion.6.refs_0_), channel_id=1, source_target_pairs={{0,4},{4,8},{8,12},{12,0},{1,5},{5,9},{9,13},{13,1},{2,6},{6,10},{... | collective-permute-start | bytes 1572872 | tf_op jit(solution)/shard_map/ppermute | solution.py:35
  13.1 14.3 %collective-permute-start.5 = (bf16[32,8192]{1,0:T(8,128)(2,1)S(1)}, bf16[32,8192]{1,0:T(8,128)(2,1)S(1)}, u32[]{:S(2)}, u32[]{:S(2)}) collective-permute-start(bf16[32,8192]{1,0:T(8,128)(2,1)S(1)} %pad_maximum_fusion.6.refs_0_), channel_id=1, source_target_pairs={{0,12},{4,0},{8,4},{12,8},{1,13},{5,1},{9,5},{13,9},{2,14},{6,2},{... | collective-permute-start | bytes 1572872 | tf_op jit(solution)/shard_map/ppermute | solution.py:35
  14.6 12.8 %collective-permute-start.6 = (bf16[32,8192]{1,0:T(8,128)(2,1)S(1)}, bf16[32,8192]{1,0:T(8,128)(2,1)S(1)}, u32[]{:S(2)}, u32[]{:S(2)}) collective-permute-start(bf16[32,8192]{1,0:T(8,128)(2,1)S(1)} %pad_maximum_fusion.6.refs_0_), channel_id=1, source_target_pairs={{0,16},{4,20},{8,24},{12,28},{1,17},{5,21},{9,25},{13,29},{2,18},{... | collective-permute-start | bytes 1572872 | tf_op jit(solution)/shard_map/ppermute | solution.py:35
  15.8 11.6 %collective-permute-start.7 = (bf16[32,8192]{1,0:T(8,128)(2,1)S(1)}, bf16[32,8192]{1,0:T(8,128)(2,1)S(1)}, u32[]{:S(2)}, u32[]{:S(2)}) collective-permute-start(bf16[32,8192]{1,0:T(8,128)(2,1)S(1)} %pad_maximum_fusion.6.refs_0_), channel_id=1, source_target_pairs={{0,80},{4,84},{8,88},{12,92},{1,81},{5,85},{9,89},{13,93},{2,82},{... | collective-permute-start | bytes 1572872 | tf_op jit(solution)/shard_map/ppermute | solution.py:35
  17.3 10.4 %collective-permute-start.3 = (bf16[32,8192]{1,0:T(8,128)(2,1)S(1)}, bf16[32,8192]{1,0:T(8,128)(2,1)S(1)}, u32[]{:S(2)}, u32[]{:S(2)}) collective-permute-start(bf16[32,8192]{1,0:T(8,128)(2,1)S(1)} %pad_maximum_fusion.6.refs_0_), channel_id=1, source_target_pairs={{0,32},{32,0},{1,33},{33,1},{2,34},{34,2},{3,35},{35,3},{4,36},{36... | collective-permute-start | bytes 1572872 | tf_op jit(solution)/shard_map/ppermute | solution.py:39
  20.2 0.8 copy-start.1
  27.8 11.3 %collective-permute-start.11 = (bf16[80,8192]{1,0:T(8,128)(2,1)S(1)}, bf16[80,8192]{1,0:T(8,128)(2,1)S(1)}, u32[]{:S(2)}, u32[]{:S(2)}) collective-permute-start(bf16[80,8192]{1,0:T(8,128)(2,1)S(1)} %get-tuple-element.33.refs_1_), channel_id=1, source_target_pairs={{0,32},{32,0},{1,33},{33,1},{2,34},{34,2},{3,35},{35,3},{4,36},{36... | collective-permute-start | bytes 3932168 | tf_op jit(solution)/shard_map/ppermute | solution.py:39
  30.5 17.2 %collective-permute-start.10 = (bf16[80,8192]{1,0:T(8,128)(2,1)S(1)}, bf16[80,8192]{1,0:T(8,128)(2,1)S(1)}, u32[]{:S(2)}, u32[]{:S(2)}) collective-permute-start(bf16[80,8192]{1,0:T(8,128)(2,1)S(1)} %get-tuple-element.34), channel_id=1, source_target_pairs={{0,12},{4,0},{8,4},{12,8},{1,13},{5,1},{9,5},{13,9},{2,14},{6,2},{... | collective-permute-start | bytes 3932168 | tf_op jit(solution)/shard_map/ppermute | solution.py:35
  31.9 18.0 %collective-permute-start.9 = (bf16[80,8192]{1,0:T(8,128)(2,1)S(1)}, bf16[80,8192]{1,0:T(8,128)(2,1)S(1)}, u32[]{:S(2)}, u32[]{:S(2)}) collective-permute-start(bf16[80,8192]{1,0:T(8,128)(2,1)S(1)} %get-tuple-element.33.refs_1_), channel_id=1, source_target_pairs={{0,4},{4,8},{8,12},{12,0},{1,5},{5,9},{9,13},{13,1},{2,6},{6,10},{... | collective-permute-start | bytes 3932168 | tf_op jit(solution)/shard_map/ppermute | solution.py:35
  32.0 7.1 %collective-permute-start.12 = (bf16[48,8192]{1,0:T(8,128)(2,1)S(1)}, bf16[48,8192]{1,0:T(8,128)(2,1)S(1)}, u32[]{:S(2)}, u32[]{:S(2)}) collective-permute-start(bf16[48,8192]{1,0:T(8,128)(2,1)S(1)} %pad_maximum_fusion.5.refs_2_), channel_id=1, source_target_pairs={{0,32},{32,0},{1,33},{33,1},{2,34},{34,2},{3,35},{35,3},{4,36},{36... | collective-permute-start | bytes 2359304 | tf_op jit(solution)/shard_map/ppermute | solution.py:39
  32.6 15.1 %collective-permute-start.8 = (bf16[32,8192]{1,0:T(8,128)(2,1)S(1)}, bf16[32,8192]{1,0:T(8,128)(2,1)S(1)}, u32[]{:S(2)}, u32[]{:S(2)}) collective-permute-start(bf16[32,8192]{1,0:T(8,128)(2,1)S(1)} %pad_maximum_fusion.6.refs_0_), channel_id=1, source_target_pairs={{0,64},{4,68},{8,72},{12,76},{1,65},{5,69},{9,73},{13,77},{2,66},{... | collective-permute-start | bytes 1572872 | tf_op jit(solution)/shard_map/ppermute | solution.py:35
  49.9 13.9 %collective-permute-start.16 = (bf16[80,8192]{1,0:T(8,128)(2,1)S(1)}, bf16[80,8192]{1,0:T(8,128)(2,1)S(1)}, u32[]{:S(2)}, u32[]{:S(2)}) collective-permute-start(bf16[80,8192]{1,0:T(8,128)(2,1)S(1)} %collective-permute-done.9.refs_0_), channel_id=1, source_target_pairs={{0,32},{32,0},{1,33},{33,1},{2,34},{34,2},{3,35},{35,3},{4,36},{36... | collective-permute-start | bytes 3932168 | tf_op jit(solution)/shard_map/ppermute | solution.py:39
  51.4 12.4 %collective-permute-start.17 = (bf16[80,8192]{1,0:T(8,128)(2,1)S(1)}, bf16[80,8192]{1,0:T(8,128)(2,1)S(1)}, u32[]{:S(2)}, u32[]{:S(2)}) collective-permute-start(bf16[80,8192]{1,0:T(8,128)(2,1)S(1)} %collective-permute-done.10.refs_1_), channel_id=1, source_target_pairs={{0,32},{32,0},{1,33},{33,1},{2,34},{34,2},{3,35},{35,3},{4,36},{36... | collective-permute-start | bytes 3932168 | tf_op jit(solution)/shard_map/ppermute | solution.py:39
  51.7 4.9 %collective-permute-start.18 = (bf16[32,8192]{1,0:T(8,128)(2,1)S(1)}, bf16[32,8192]{1,0:T(8,128)(2,1)S(1)}, u32[]{:S(2)}, u32[]{:S(2)}) collective-permute-start(bf16[32,8192]{1,0:T(8,128)(2,1)S(1)} %collective-permute-done.8.refs_2_), channel_id=1, source_target_pairs={{0,32},{32,0},{1,33},{33,1},{2,34},{34,2},{3,35},{35,3},{4,36},{36... | collective-permute-start | bytes 1572872 | tf_op jit(solution)/shard_map/ppermute | solution.py:39
  52.6 18.7 %collective-permute-start.13 = (bf16[64,8192]{1,0:T(8,128)(2,1)S(1)}, bf16[64,8192]{1,0:T(8,128)(2,1)S(1)}, u32[]{:S(2)}, u32[]{:S(2)}) collective-permute-start(bf16[64,8192]{1,0:T(8,128)(2,1)S(1)} %get-tuple-element.53), channel_id=1, source_target_pairs={{0,4},{4,8},{8,12},{12,0},{1,5},{5,9},{9,13},{13,1},{2,6},{6,10},{... | collective-permute-start | bytes 3145736 | tf_op jit(solution)/shard_map/ppermute | solution.py:35
  52.7 18.6 %collective-permute-start.14 = (bf16[64,8192]{1,0:T(8,128)(2,1)S(1)}, bf16[64,8192]{1,0:T(8,128)(2,1)S(1)}, u32[]{:S(2)}, u32[]{:S(2)}) collective-permute-start(bf16[64,8192]{1,0:T(8,128)(2,1)S(1)} %get-tuple-element.52), channel_id=1, source_target_pairs={{0,12},{4,0},{8,4},{12,8},{1,13},{5,1},{9,5},{13,9},{2,14},{6,2},{... | collective-permute-start | bytes 3145736 | tf_op jit(solution)/shard_map/ppermute | solution.py:35
  56.7 14.6 %collective-permute-start.15 = (bf16[32,8192]{1,0:T(8,128)(2,1)S(1)}, bf16[32,8192]{1,0:T(8,128)(2,1)S(1)}, u32[]{:S(2)}, u32[]{:S(2)}) collective-permute-start(bf16[32,8192]{1,0:T(8,128)(2,1)S(1)} %pad_maximum_fusion.7), channel_id=1, source_target_pairs={{0,64},{4,68},{8,72},{12,76},{1,65},{5,69},{9,73},{13,77},{2,66},{... | collective-permute-start | bytes 1572872 | tf_op jit(solution)/shard_map/ppermute | solution.py:35
  71.3 5.7 %collective-permute-start.19 = (bf16[64,8192]{1,0:T(8,128)(2,1)S(1)}, bf16[64,8192]{1,0:T(8,128)(2,1)S(1)}, u32[]{:S(2)}, u32[]{:S(2)}) collective-permute-start(bf16[64,8192]{1,0:T(8,128)(2,1)S(1)} %collective-permute-done.13.refs_0_), channel_id=1, source_target_pairs={{0,32},{32,0},{1,33},{33,1},{2,34},{34,2},{3,35},{35,3},{4,36},{36... | collective-permute-start | bytes 3145736 | tf_op jit(solution)/shard_map/ppermute | solution.py:39
  72.5 4.5 %collective-permute-start.20 = (bf16[64,8192]{1,0:T(8,128)(2,1)S(1)}, bf16[64,8192]{1,0:T(8,128)(2,1)S(1)}, u32[]{:S(2)}, u32[]{:S(2)}) collective-permute-start(bf16[64,8192]{1,0:T(8,128)(2,1)S(1)} %collective-permute-done.14.refs_1_), channel_id=1, source_target_pairs={{0,32},{32,0},{1,33},{33,1},{2,34},{34,2},{3,35},{35,3},{4,36},{36... | collective-permute-start | bytes 3145736 | tf_op jit(solution)/shard_map/ppermute | solution.py:39
  72.6 4.4 %collective-permute-start.21 = (bf16[32,8192]{1,0:T(8,128)(2,1)S(1)}, bf16[32,8192]{1,0:T(8,128)(2,1)S(1)}, u32[]{:S(2)}, u32[]{:S(2)}) collective-permute-start(bf16[32,8192]{1,0:T(8,128)(2,1)S(1)} %collective-permute-done.15.refs_2_), channel_id=1, source_target_pairs={{0,32},{32,0},{1,33},{33,1},{2,34},{34,2},{3,35},{35,3},{4,36},{36... | collective-permute-start | bytes 1572872 | tf_op jit(solution)/shard_map/ppermute | solution.py:39
